TPU v7x, 512 devices: a whole 4x8x8 slice. The times are simulated.
512 devices in a mesh: section: 16 (over x, y_hi, core), tp: 32 (over y_lo, z).
Axes of the slice: x: 4, y: 8 (y_hi: 2, y_lo: 4; y = y_hi * 4 + y_lo), z: 8, core: 2. Of those that a mesh axis runs over, the one named last changes fastest.
Arguments:
- hidden: bfloat16 [208, 4608], P('section', 'tp'), as said below
- head_weight: bfloat16 [4608, 131072], P(None, ('section', 'tp')), as said below
- targets: int32 [208], replicated, may hold values from 0 to 131071
Outputs:
- loss: float32 [], replicated
- head_grad: bfloat16 [4608, 131072], P(None, ('section', 'tp'))
- hidden_grad: bfloat16 [208, 4608], P('section', 'tp')
Inputs may be any that keep to these rules, and one draw needn't show every extreme that they name: hidden is drawn as independent normal entries. head_weight has entries of order 3 / sqrt(4608) and may be aligned with rows of hidden.
All inputs are finite; a program needn't handle non-finite values.
Results may differ from a plain program's by a relative error of at most 0.0051.
Values may be sent and summed in bfloat16 or wider, within the bound.
A program may use at most 64 MiB of HBM per device.

v0:
```python
import jax
import jax.numpy as jnp
from jax import lax
from jax.sharding import PartitionSpec as P


def per_device(hidden, head_weight, targets):
    vocab_dev = head_weight.shape[1]
    offset = (lax.axis_index("section") * lax.axis_size("tp") + lax.axis_index("tp")) * vocab_dev
    columns = lax.all_gather(hidden, "tp", axis=1, tiled=True)
    full_states = lax.all_gather(columns, "section", axis=0, tiled=True)
    logits = jnp.dot(full_states, head_weight, preferred_element_type=jnp.float32)
    local_top = jnp.max(logits, axis=1)
    vocab_ids = jnp.arange(vocab_dev, dtype=jnp.int32) + offset
    hit = vocab_ids[None, :] == targets[:, None]
    local_pick = jnp.sum(jnp.where(hit, logits, jnp.float32(0.0)), axis=1)
    top = lax.pmax(local_top, ("section", "tp"))
    shifted = jnp.exp(logits - top[:, None])
    total, picked = lax.psum((jnp.sum(shifted, axis=1), local_pick), ("section", "tp"))
    loss = jnp.mean(top + jnp.log(total) - picked)
    ratio = shifted / total[:, None]
    probs = ratio.astype(jnp.bfloat16)
    dlogits = (ratio - hit.astype(jnp.float32)).astype(jnp.bfloat16)
    head_grad = lax.dot_general(
        full_states, probs, (((0,), (0,)), ((), ())), preferred_element_type=jnp.float32
    ).astype(jnp.bfloat16)
    whole_terms = lax.dot_general(
        dlogits, head_weight, (((1,), (1,)), ((), ())), preferred_element_type=jnp.float32
    )
    feature_part = lax.psum_scatter(whole_terms, "tp", scatter_dimension=1, tiled=True)
    summed = lax.psum_scatter(feature_part, "section", scatter_dimension=0, tiled=True)
    return (loss, head_grad, summed.astype(jnp.bfloat16))


def solution(mesh):
    placed = (P("section", "tp"), P(None, ("section", "tp")), P())
    return jax.shard_map(
        per_device,
        mesh=mesh,
        in_specs=placed,
        out_specs=(P(), P(None, ("section", "tp")), P("section", "tp")),
        check_vma=False,
    )
```

profile of v0, /device:TPU:6, one launch (start us, length us, event | category | flops | bytes accessed | tf_op | source)
XLA Modules:
  0.0 610.2 jit_solution(17123272261160298530)
XLA Ops:
  7.2 0.0 copy-start
  7.2 0.0 all-gather.4.cloned.1.call-start
  7.2 86.6 %all-gather = bf16[32,144,13]{1,2,0:T(8,128)(2,1)S(1)} all-gather(bf16[1,144,13]{1,2,0:T(8,128)(2,1)} %bitcast.18), channel_id=1, replica_groups=mesh['section'=16,'tp'=32] {'tp'}, dimensions={0}, use_global_device_ids=true | all-gather | bytes 123552 | tf_op jit(solution)/shard_map/all_gather | solution.py:10
  93.8 0.1 copy.11
  93.9 1.0 reshape.14
  94.9 0.0 all-gather.4.cloned.1.call-update
  94.9 0.0 reduce-scatter.3.cloned.1.call-start
  95.0 59.5 %all-gather.4.cloned.1.call-done = bf16[16,13,4608]{2,1,0:T(8,128)(2,1)} async-done(((bf16[1,13,4608]{2,1,0:T(8,128)(2,1)}), bf16[16,13,4608]{2,1,0:T(8,128)(2,1)}) %all-gather.4.cloned.1.call-update) | async-done | bytes 1916944 | tf_op jit(solution)/shard_map/all_gather | solution.py:11
  154.4 2.9 reshape.16
  157.3 0.0 copy-done
  157.3 2.3 fusion.13
  159.6 99.6 %pmax.7 = f32[208]{0:T(256)S(1)} all-reduce(f32[208]{0:T(256)S(1)} %get-tuple-element.16), channel_id=1, replica_groups=mesh['section'=16,'tp'=32] {'section','tp'}, use_global_device_ids=true, to_apply=%region_1.2 | all-reduce | flops 208 | bytes 1664 | tf_op jit(solution)/shard_map/pmax | solution.py:17
  259.2 0.2 fusion.5
  259.4 94.8 %all-reduce.1 = (f32[208]{0:T(256)S(1)}, f32[208]{0:T(256)S(1)}) all-reduce(f32[208]{0:T(256)S(1)} %get-tuple-element.13, f32[208]{0:T(256)S(1)} %get-tuple-element.12), channel_id=1, replica_groups=mesh['section'=16,'tp'=32] {'section','tp'}, use_global_device_ids=true, to_apply=%region_5.6 | all-reduce | flops 416 | bytes 3328 | tf_op jit(solution)/shard_map/psum | solution.py:19
  354.2 3.0 fusion.6
  357.2 0.0 reduce-scatter.3.cloned.1.call-update
  357.3 1.3 dynamic-slice
  359.2 3.9 fusion
  363.1 4.3 copy.12
  367.3 0.6 subtract_reduce_fusion
  368.6 156.1 %reduce-scatter.3.cloned.1.call-done = f32[208,144]{0,1:T(8,128)} async-done(((f32[208,4608]{0,1:T(8,128)}), f32[208,144]{0,1:T(8,128)}) %reduce-scatter.3.cloned.1.call-update) | async-done | bytes 119824 | tf_op jit(solution)/shard_map/reduce_scatter | solution.py:30
  524.7 76.7 %all-reduce = bf16[208,144]{0,1:T(8,128)(2,1)S(1)} all-reduce(f32[208,144]{0,1:T(8,128)} %reduce-scatter.3.cloned.1.call-done), channel_id=3, replica_groups=mesh['section'=16,'tp'=32] {'section'}, use_global_device_ids=true, to_apply=%region_8.9.clone | all-reduce | flops 29952 | bytes 179712
  601.4 0.1 dynamic-slice_convert_fusion
  601.5 0.7 copy.13
  (3 shorter events, 0.0 us)
Async XLA Ops:
  7.2 150.2 %copy-start = (bf16[4608,256]{1,0:T(8,128)(2,1)S(1)}, bf16[4608,256]{1,0:T(8,128)(2,1)}, u32[]{:S(2)}) copy-start(bf16[4608,256]{1,0:T(8,128)(2,1)} %param.4) | copy-start | bytes 7077892
  7.2 147.2 %all-gather.4.cloned.1.call-start = ((), (), s32[]{:S(2)}) async-start(), calls=%async_computation.2 | async-start | bytes 2506752 | tf_op jit(solution)/shard_map/all_gather | solution.py:11
  94.9 429.8 %reduce-scatter.3.cloned.1.call-start = ((), (), s32[]{:S(2)}) async-start(), calls=%async_computation.1 | async-start | bytes 4866048 | tf_op jit(solution)/shard_map/reduce_scatter | solution.py:30
  157.3 101.9 %copy-start.1 = (s32[208]{0:T(256)S(1)}, s32[208]{0:T(256)}, u32[]{:S(2)}) copy-start(s32[208]{0:T(256)} %param.5) | copy-start | bytes 2500
Sparse Core Ops, SparseCore 0:
  95.0 59.3 all-gather.3
  357.4 167.3 reduce-scatter.2
where the time goes:
time: 614 us; the launch traced here: 610 us
  blocking collectives  358 us (58%)
  waiting for transfers between devices  216 us (35%)
  between operations  16.5 us (3%)
  local copies, waits for them, and re-layouts  10.3 us (2%)
  matrix products  9.21 us (2%)
    reduce_scatter x1, waiting for transfers between devices, per_device(): lax.psum_scatter(whole_terms, 'tp', scatter_dimension=1, tiled=True)  156 us
    pmax x1, blocking collectives, per_device(): top = lax.pmax(local_top, ('section', 'tp'))  99.6 us
    psum x1, blocking collectives, per_device(): lax.psum((jnp.sum(shifted, axis=1), local_pick), ('section', 'tp'))  94.8 us
    all_gather x1, blocking collectives, per_device(): columns = lax.all_gather(hidden, 'tp', axis=1, tiled=True)  86.6 us
    unnamed x1, blocking collectives  76.7 us
    all_gather x1, waiting for transfers between devices, per_device(): full_states = lax.all_gather(columns, 'section', axis=0, tiled=True)  59.5 us
  transfers between devices with their start and end apart: 2, of which 2 were waited for; matrix products, arithmetic and copies ran while one was open for 2% of the time, Pallas kernels for 0%

commit v1 on v0

v1 whole, which is shorter than its diff:
```python
import functools

import jax
import jax.numpy as jnp
from jax import lax
from jax.experimental import pallas as pl
from jax.experimental.pallas import tpu as pltpu
from jax.sharding import PartitionSpec as P

MESH = pl.DeviceIdType.MESH
F32 = jnp.float32
BF16 = jnp.bfloat16
NX, NY, NZ, NC = 4, 8, 8, 2
YL = 4
ROWS = 13
PAD = 16
FEATS = 144
COLS = NZ * FEATS
BLOCKS = 16
TALL = BLOCKS * PAD
HALF = TALL // 2
D = YL * COLS
VOCAB_DEV = 256
TOKENS = 208
ORDER = (1, 7, 2, 6, 3, 5, 4)
XORDER = (1, 3, 2)


def kernel(shard, weight_hbm, targets, loss, head_grad, hidden_grad,
           weight, hid, pad32, own, zrec, line32, stat, st_x, st_y, st_z, keep, c_out, c_in, x_out, x_in,
           y_out, y_in, z_out, z_in, grad, wsem, gsem, bs, br,
           zs, zr, ys, yr, xs, xr, cs, cr, ss, sr, rcs, rcr, rxs, rxr, rys, ryr, rzs, rzr):
    s = lax.axis_index("section")
    t = lax.axis_index("tp")
    x, yh, c = s // 4, (s // 2) % 2, s % 2
    yl, z = t // NZ, t % NZ
    y = yh * YL + yl

    def at(x_, y_, z_, c_):
        return {"section": x_ * 4 + (y_ // YL) * 2 + c_, "tp": (y_ % YL) * NZ + z_}

    def z_peer(d):
        return at(x, y, (z + d) % NZ, c)

    def y_peer(d):
        return at(x, (y + d) % NY, z, c)

    def x_peer(d, dc=0):
        return at((x + d) % NX, y, z, (c + dc) % 2)

    def remote(src, dst, send, recv, peer):
        return pltpu.make_async_remote_copy(
            src_ref=src, dst_ref=dst, send_sem=send, recv_sem=recv, device_id=peer, device_id_type=MESH)

    sent = []

    def go(copy):
        copy.start()
        sent.append(copy)
        return copy

    fetch = pltpu.make_async_copy(weight_hbm, weight, wsem)
    fetch.start()

    xc = [(d, dc) for d in range(NX) for dc in range(NC) if d or dc]
    peers = [z_peer(d) for d in ORDER] + [y_peer(d) for d in ORDER] + [x_peer(d, dc) for d, dc in xc]
    barrier = pltpu.get_barrier_semaphore()
    for peer in peers:
        pl.semaphore_signal(barrier, inc=1, device_id=peer, device_id_type=MESH)

    pad32[...] = jnp.zeros_like(pad32)
    pad32[0:ROWS, 0:FEATS] = shard[...].astype(F32)
    mine = pad32[...].astype(BF16)
    own[...] = mine
    pl.semaphore_wait(barrier, len(peers))

    copies = [go(remote(own, zrec.at[z], zs.at[d], zr.at[d], z_peer(d))) for d in ORDER]
    zrec[z] = mine
    for copy in copies:
        copy.wait_recv()
    for i in range(NZ):
        line32[:, FEATS * i:FEATS * (i + 1)] = zrec[i][:, 0:FEATS].astype(F32)

    def place(x_, y_, c_):
        rows = pl.ds(pl.multiple_of((c_ * 8 + x_ * 2 + y_ // YL) * PAD, PAD), PAD)
        cols = pl.ds(pl.multiple_of((y_ % YL) * COLS, 128), COLS)
        return hid.at[rows, cols]

    place(x, y, c)[...] = line32[...].astype(BF16)

    ycopies = {d: go(remote(place(x, y, c), place(x, y, c), ys.at[d], yr.at[d], y_peer(d))) for d in ORDER}
    partner = x_peer(0, 1)
    xcopies = []
    ccopies = []
    for d in (0,) + ORDER:
        if d:
            ycopies[d].wait_recv()
        from_y = (y + NY - d) % NY
        block = place(x, from_y, c)
        for dx in XORDER:
            n = d * NX + dx
            xcopies.append((d, dx, go(remote(block, block, xs.at[n], xr.at[n], x_peer(dx)))))
        ccopies.append(go(remote(block, block, cs.at[d * NX], cr.at[d * NX], partner)))
    for d, dx, copy in xcopies:
        copy.wait_recv()
        block = place((x + NX - dx) % NX, (y + NY - d) % NY, c)
        n = d * NX + dx
        ccopies.append(go(remote(block, block, cs.at[n], cr.at[n], partner)))
    for copy in ccopies:
        copy.wait_recv()
    fetch.wait()

    def cols_of(j):
        return pl.ds(pl.multiple_of(j * COLS, 128), COLS)

    logits = lax.fori_loop(
        0, YL, lambda j, acc: acc + jnp.dot(hid[:, cols_of(j)], weight[cols_of(j), :], preferred_element_type=F32),
        jnp.zeros((TALL, VOCAB_DEV), F32))
    top = jnp.max(logits, axis=1, keepdims=True)
    shifted = jnp.exp(logits - top)
    total = jnp.sum(shifted, axis=1, keepdims=True)
    row = lax.broadcasted_iota(jnp.int32, (TALL, TOKENS), 0)
    b = row // PAD
    token = ((b // 2) % 4 * 4 + b % 2 * 2 + b // 8) * ROWS + row % PAD
    match = (token == lax.broadcasted_iota(jnp.int32, (TALL, TOKENS), 1)) & (row % PAD < ROWS)
    goal = jnp.sum(jnp.where(match, targets[...].astype(F32), 0.0), axis=1, keepdims=True).astype(jnp.int32)
    vocab = lax.broadcasted_iota(jnp.int32, (TALL, VOCAB_DEV), 1) + (s * (YL * NZ) + t) * VOCAB_DEV
    hit = vocab == goal
    picked = jnp.sum(jnp.where(hit, logits, 0.0), axis=1, keepdims=True)

    lane = lax.broadcasted_iota(jnp.int32, (TALL, 128), 1)
    wide = jnp.where(lane == 0, top, jnp.where(lane == 1, total, jnp.where(lane == 2, picked, 0.0)))
    stat[0] = wide.T[0:8, :]

    def merge(parts):
        best = functools.reduce(jnp.maximum, [p[0:1, :] for p in parts])
        amount = sum(p[1:2, :] * jnp.exp(p[0:1, :] - best) for p in parts)
        pick = sum(p[2:3, :] for p in parts)
        return jnp.concatenate([best, amount, pick, jnp.zeros((5, TALL), F32)], axis=0)

    k = 0
    for stage, (buf, targets_of) in enumerate((
            (st_x, [x_peer(d, dc) for d, dc in xc]),
            (st_y, [y_peer(d) for d in ORDER]),
            (st_z, [z_peer(d) for d in ORDER]))):
        copies = []
        for i, peer in enumerate(targets_of):
            copies.append(go(remote(stat.at[stage], buf.at[i], ss.at[k], sr.at[k], peer)))
            k += 1
        for copy in copies:
            copy.wait_recv()
        stat[stage + 1] = merge([stat[stage]] + [buf[i] for i in range(len(targets_of))])

    final = stat[3]
    slot = lax.broadcasted_iota(jnp.int32, (1, TALL), 1)
    each = jnp.where(slot % PAD < ROWS, final[0:1, :] + jnp.log(final[1:2, :]) - final[2:3, :], 0.0)
    loss[0, 0] = jnp.sum(each) / TOKENS

    back = jnp.concatenate([final, jnp.zeros((120, TALL), F32)], axis=0).T
    ratio = shifted * jnp.exp(top - back[:, 0:1]) / back[:, 1:2]
    probs = ratio.astype(BF16)
    dlogits = (ratio - hit.astype(F32)).astype(BF16)

    ccopies = []
    for j in range(YL):
        cols = pl.ds(j * COLS, COLS)
        terms = lax.dot_general(dlogits, weight[cols, :], (((1,), (1,)), ((), ())), preferred_element_type=F32)
        first, second = terms[0:HALF], terms[HALF:TALL]
        is0 = c == 0
        keep[:, cols] = jnp.where(is0, first, second)
        c_out[:, cols] = jnp.where(is0, second, first).astype(BF16)
        ccopies.append(go(remote(c_out.at[:, cols], c_in.at[:, cols], rcs.at[j], rcr.at[j], partner)))
    rxcopies = []
    for j in range(YL):
        cols = pl.ds(j * COLS, COLS)
        ccopies[j].wait_recv()
        both = keep[:, cols] + c_in[:, cols].astype(F32)
        keep[:, cols] = both
        x_out[:, cols] = both.astype(BF16)
        for dx in XORDER:
            n = j * NX + dx
            rows = pl.ds(pl.multiple_of((x + dx) % NX * 32, 32), 32)
            rxcopies.append(go(remote(x_out.at[rows, cols], x_in.at[dx, :, cols], rxs.at[n], rxr.at[n], x_peer(dx))))

    writes = []
    for j in range(YL):
        cols = pl.ds(j * COLS, COLS)
        grad[cols, :] = lax.dot_general(
            hid[:, cols], probs, (((0,), (0,)), ((), ())), preferred_element_type=F32).astype(BF16)
        write = pltpu.make_async_copy(grad.at[cols, :], head_grad.at[cols, :], gsem.at[j])
        write.start()
        writes.append(write)

    my_x = pl.ds(pl.multiple_of(x * 32, 32), 32)
    for j in range(YL):
        cols = pl.ds(j * COLS, COLS)
        for copy in rxcopies[j * 3:j * 3 + 3]:
            copy.wait_recv()
        y_out[:, cols] = (keep[my_x, cols] + x_in[1, :, cols].astype(F32) + x_in[2, :, cols].astype(F32)
                          + x_in[3, :, cols].astype(F32)).astype(BF16)

    def y_part(y_):
        rows = pl.ds(pl.multiple_of(y_ // YL * PAD, PAD), PAD)
        cols = pl.ds(pl.multiple_of((y_ % YL) * COLS, 128), COLS)
        return y_out.at[rows, cols]

    copies = [go(remote(y_part((y + d) % NY), y_in.at[d], rys.at[d], ryr.at[d], y_peer(d))) for d in ORDER]
    total_y = y_part(y)[...].astype(F32)
    for d, copy in zip(ORDER, copies):
        copy.wait_recv()
        total_y = total_y + y_in[d].astype(F32)
    for i in range(NZ):
        z_out[i, :, 0:FEATS] = total_y[:, FEATS * i:FEATS * (i + 1)]
    copies = [go(remote(z_out.at[(z + d) % NZ], z_in.at[d], rzs.at[d], rzr.at[d], z_peer(d))) for d in ORDER]
    result = z_out[z][:, 0:FEATS]
    for d, copy in zip(ORDER, copies):
        copy.wait_recv()
        result = result + z_in[d][:, 0:FEATS]
    hidden_grad[...] = result[0:ROWS].astype(BF16)

    for copy in sent:
        copy.wait_send()
    for write in writes:
        write.wait()


def per_device(hidden, head_weight, targets):
    vmem = pl.BlockSpec(memory_space=pltpu.VMEM)
    hbm = pl.BlockSpec(memory_space=pl.ANY)
    dma = pltpu.SemaphoreType.DMA
    loss, head_grad, hidden_grad = pl.pallas_call(
        kernel,
        out_shape=(
            jax.ShapeDtypeStruct((1, 1), F32),
            jax.ShapeDtypeStruct((D, VOCAB_DEV), BF16),
            jax.ShapeDtypeStruct((ROWS, FEATS), BF16),
        ),
        in_specs=[vmem, hbm, vmem],
        out_specs=(pl.BlockSpec(memory_space=pltpu.SMEM), hbm, vmem),
        scratch_shapes=[
            pltpu.VMEM((D, VOCAB_DEV), BF16),
            pltpu.VMEM((TALL, D), BF16),
            pltpu.VMEM((PAD, 256), F32),
            pltpu.VMEM((PAD, 256), BF16),
            pltpu.VMEM((NZ, PAD, 256), BF16),
            pltpu.VMEM((PAD, COLS), F32),
            pltpu.VMEM((4, 8, TALL), F32),
            pltpu.VMEM((7, 8, TALL), F32),
            pltpu.VMEM((7, 8, TALL), F32),
            pltpu.VMEM((7, 8, TALL), F32),
            pltpu.VMEM((HALF, D), F32),
            pltpu.VMEM((HALF, D), BF16),
            pltpu.VMEM((HALF, D), BF16),
            pltpu.VMEM((HALF, D), BF16),
            pltpu.VMEM((NX, 32, D), BF16),
            pltpu.VMEM((32, D), BF16),
            pltpu.VMEM((NY, PAD, COLS), BF16),
            pltpu.VMEM((NZ, PAD, 256), F32),
            pltpu.VMEM((NZ, PAD, 256), F32),
            pltpu.VMEM((D, VOCAB_DEV), BF16),
            dma, dma((YL,)), dma, dma,
            dma((8,)), dma((8,)), dma((8,)), dma((8,)),
            dma((32,)), dma((32,)), dma((32,)), dma((32,)),
            dma((21,)), dma((21,)), dma((YL,)), dma((YL,)),
            dma((16,)), dma((16,)), dma((8,)), dma((8,)), dma((8,)), dma((8,)),
        ],
        compiler_params=pltpu.CompilerParams(
            collective_id=0, has_side_effects=True, vmem_limit_bytes=48 * 2**20),
        name="output_layer",
    )(hidden, head_weight, targets.reshape(1, TOKENS))
    return loss.reshape(()), head_grad, hidden_grad


def solution(mesh):
    placed = (P("section", "tp"), P(None, ("section", "tp")), P())
    return jax.shard_map(
        per_device,
        mesh=mesh,
        in_specs=placed,
        out_specs=(P(), P(None, ("section", "tp")), P("section", "tp")),
        check_vma=False,
    )
```

time: 614 us -> 93.6 us (0.15)
  blocking collectives: 358 us -> 0 us
  waiting for transfers between devices: 216 us -> 0 us
  Pallas kernels: 0 us -> 85 us
  between operations: 16.5 us -> 2.38 us
  matrix products: 9.21 us -> 0 us
    reduce_scatter x1 -> x0, waiting for transfers between devices: 156 us -> none  [per_device(): lax.psum_scatter(whole_terms, 'tp', scatter_dimension=1, tiled=True)]
    pmax x1 -> x0, blocking collectives: 99.6 us -> none  [per_device(): top = lax.pmax(local_top, ('section', 'tp'))]
    psum x1 -> x0, blocking collectives: 94.8 us -> none  [per_device(): lax.psum((jnp.sum(shifted, axis=1), local_pick), ('section', 'tp'))]
    all_gather x1 -> x0, blocking collectives: 86.6 us -> none  [per_device(): columns = lax.all_gather(hidden, 'tp', axis=1, tiled=True)]
    pallas_call x0 -> x1, Pallas kernels: none -> 85 us  [per_device(): pl.pallas_call(kernel, out_shape=(jax.ShapeDtypeStruct((1, 1), F32), jax....]
    unnamed x1 -> x0, blocking collectives: 76.7 us -> none
    all_gather x1 -> x0, waiting for transfers between devices: 59.5 us -> none  [per_device(): full_states = lax.all_gather(columns, 'section', axis=0, tiled=True)]
    dot_general x3 -> x0, matrix products: 9.21 us -> none  [the longest x1 3.89 us: per_device(): lax.dot_general(full_states, probs, (((0,), (0,)), ((), ())), preferred_e...]
  transfers between devices with their start and end apart: 2 -> 0, of which waited for: 2 -> 0; matrix products, arithmetic and copies ran while one was open for 2% -> 0% of each run, Pallas kernels for 0% -> 0%
where the time goes in v1:
time: 93.6 us; the launch traced here: 92.4 us
  Pallas kernels  85 us (91%)
  local copies, waits for them, and re-layouts  5.04 us (5%)
  between operations  2.38 us (3%)
    pallas_call x1, Pallas kernels, per_device(): pl.pallas_call(kernel, out_shape=(jax.ShapeDtypeStruct((1, 1), F32), jax....  85 us
    unnamed x8, local copies, waits for them, and re-layouts  5.04 us

profile of v1, /device:TPU:6, one launch (start us, length us, event | category | flops | bytes accessed | tf_op | source)
XLA Modules:
  0.0 92.4 jit_solution(11470450904170344749)
XLA Ops:
  0.6 0.0 copy-start
  0.6 1.7 %copy-done = bf16[4608,256]{1,0:T(8,128)(2,1)S(1)} copy-done((bf16[4608,256]{1,0:T(8,128)(2,1)S(1)}, bf16[4608,256]{1,0:T(8,128)(2,1)}, u32[]{:S(2)}) %copy-start) | copy-done | bytes 2359320
  2.3 0.0 copy-start.1
  2.3 0.7 copy-done.1
  3.0 0.0 copy-start.2
  3.0 0.7 copy-done.2
  3.7 85.0 %output_layer.1 = (f32[1,1]{1,0:T(1,128)}, bf16[4608,256]{1,0:T(8,128)(2,1)S(1)}, bf16[13,144]{1,0:T(8,128)(2,1)S(1)}) custom-call(bf16[13,144]{1,0:T(8,128)(2,1)S(1)} %copy-done.1, bf16[4608,256]{1,0:T(8,128)(2,1)S(1)} %copy-done, s32[1,208]{1,0:T(1,128)S(1)} %bitcast.2), custom_call_target="tpu_custom_call" | custom-call | tf_op jit(solution)/shard_map/output_layer/pallas_call | solution.py:231
  89.3 1.4 %copy.10 = bf16[4608,256]{1,0:T(8,128)(2,1)} copy(bf16[4608,256]{1,0:T(8,128)(2,1)S(1)} %get-tuple-element.13) | data formatting | bytes 4718592
  90.7 0.6 copy.11
Async XLA Ops:
  0.6 1.7 %copy-start = (bf16[4608,256]{1,0:T(8,128)(2,1)S(1)}, bf16[4608,256]{1,0:T(8,128)(2,1)}, u32[]{:S(2)}) copy-start(bf16[4608,256]{1,0:T(8,128)(2,1)} %weight_hbm.1) | copy-start | bytes 7077892
  2.3 0.7 copy-start.1
  3.0 0.7 copy-start.2

commit v2 on v0

v2 whole, which is shorter than its diff:
```python
import functools

import jax
import jax.numpy as jnp
from jax import lax
from jax.experimental import pallas as pl
from jax.experimental.pallas import tpu as pltpu
from jax.sharding import PartitionSpec as P

MESH = pl.DeviceIdType.MESH
F32 = jnp.float32
BF16 = jnp.bfloat16
NX, NY, NZ, NC = 4, 8, 8, 2
YH, YL = 2, 4
ROWS = 13
PAD = 16
FEATS = 144
FA, FB, FC = 80, 32, 32
WA, WB, WC = NZ * FA, NZ * FB, YL * FC
HALF = YH * NX * PAD
TALL = NC * HALF
D = YL * NZ * FEATS
VOCAB_DEV = 256
TOKENS = 208
ORDER = (1, 7, 2, 6, 3, 5, 4)
XORDER = (1, 3, 2)


def kernel(shard_hbm, weight_hbm, targets_hbm, loss, head_grad, hidden_grad,
           shard, targets, w_a, w_b, w_c, hid_a, hid_b, hid_c, pad32, own_ab, own_c, z_rec, y_rec,
           line_a, line_b, line_c, stat, st_x, st_y, st_z,
           keep_a, keep_b, keep_c, out_a, out_b, out_c, in_a, in_b, in_c,
           s1_a, s1_b, s1_c, r1_a, r1_b, r1_c, s2_a, s2_b, s2_c, r2_a, r2_b, r2_c,
           s3_ab, s3_c, r3_ab, r3_c, g_a, g_b, g_c, local, gsem, ssem, rsem):
    s = lax.axis_index("section")
    t = lax.axis_index("tp")
    x, yh, c = s // 4, (s // 2) % 2, s % 2
    yl, z = t // NZ, t % NZ
    y = yh * YL + yl

    def at(x_, y_, z_, c_):
        return {"section": x_ * 4 + (y_ // YL) * 2 + c_, "tp": (y_ % YL) * NZ + z_}

    def z_peer(d):
        return at(x, y, (z + d) % NZ, c)

    def y_peer(d):
        return at(x, (y + d) % NY, z, c)

    def x_peer(d, dc=0):
        return at((x + d) % NX, y, z, (c + dc) % 2)

    sent = []

    def go(src, dst, peer):
        n = len(sent)
        copy = pltpu.make_async_remote_copy(
            src_ref=src, dst_ref=dst, send_sem=ssem.at[n], recv_sem=rsem.at[n], device_id=peer, device_id_type=MESH)
        copy.start()
        sent.append(copy)
        return copy

    fetch_small = [
        pltpu.make_async_copy(shard_hbm, shard, local.at[0]),
        pltpu.make_async_copy(targets_hbm, targets, local.at[1]),
    ]
    fetch = [
        pltpu.make_async_copy(weight_hbm.at[:, :, 0:FA], w_a, local.at[2]),
        pltpu.make_async_copy(weight_hbm.at[:, :, FA:FA + FB], w_b, local.at[3]),
    ] + [
        pltpu.make_async_copy(weight_hbm.at[:, i, FA + FB:FEATS], w_c.at[i], local.at[4 + i]) for i in range(NZ)
    ]
    for copy in fetch_small + fetch:
        copy.start()

    xc = [(d, dc) for d in range(NX) for dc in range(NC) if d or dc]
    peers = [z_peer(d) for d in ORDER] + [y_peer(d) for d in ORDER] + [x_peer(d, dc) for d, dc in xc]
    barrier = pltpu.get_barrier_semaphore()
    for peer in peers:
        pl.semaphore_signal(barrier, inc=1, device_id=peer, device_id_type=MESH)

    for copy in fetch_small:
        copy.wait()
    pad32[...] = jnp.zeros_like(pad32)
    pad32[0, 0:ROWS, 0:FA + FB] = shard[:, 0:FA + FB].astype(F32)
    pad32[1, 0:ROWS, 0:FC] = shard[:, FA + FB:FEATS].astype(F32)
    mine_ab, mine_c = pad32[0].astype(BF16), pad32[1].astype(BF16)
    own_ab[...] = mine_ab
    own_c[...] = mine_c
    pl.semaphore_wait(barrier, len(peers))

    z_copies = [go(own_ab, z_rec.at[z], z_peer(d)) for d in ORDER]
    y_copies = [go(own_c, y_rec.at[y], y_peer(d)) for d in ORDER]
    z_rec[z] = mine_ab
    y_rec[y] = mine_c
    for copy in z_copies:
        copy.wait_recv()
    for i in range(NZ):
        part = z_rec[i].astype(F32)
        line_a[:, FA * i:FA * (i + 1)] = part[:, 0:FA]
        line_b[:, FB * i:FB * (i + 1)] = part[:, FA:FA + FB]
    hid_a[yl, 0, yh, x] = line_a[...].astype(BF16)
    hid_b[yl, 0, yh, x] = line_b[...].astype(BF16)

    partner = x_peer(0, 1)
    block = hid_a.at[yl, 0, yh, x]
    a_y = {d: go(block, block, y_peer(d)) for d in ORDER}
    block = hid_b.at[yl, 0, yh, x]
    b_x = [go(block, block, x_peer(d)) for d in XORDER]
    for copy in y_copies:
        copy.wait_recv()
    for i in range(NY):
        line_c[i // YL, :, FC * (i % YL):FC * (i % YL + 1)] = y_rec[i].astype(F32)[:, 0:FC]
    hid_c[z, 0, :, x] = line_c[...].astype(BF16)
    block = hid_c.at[z, 0, :, x]
    c_x = [go(block, block, x_peer(d)) for d in XORDER]

    across = []
    a_x = []

    def pass_a(d):
        from_y = (y + NY - d) % NY
        block = hid_a.at[from_y % YL, 0, from_y // YL, x]
        for dx in XORDER:
            a_x.append((d, dx, go(block, block, x_peer(dx))))
        across.append(go(block, hid_a.at[from_y % YL, 1, from_y // YL, x], partner))

    pass_a(0)
    for copy in b_x:
        copy.wait_recv()
    block = hid_b.at[yl, 0, yh]
    b_y = [(d, go(block, block, y_peer(d))) for d in ORDER]
    across.append(go(block, hid_b.at[yl, 1, yh], partner))
    for copy in c_x:
        copy.wait_recv()
    block = hid_c.at[z, 0]
    c_z = [(d, go(block, block, z_peer(d))) for d in ORDER]
    across.append(go(block, hid_c.at[z, 1], partner))
    for d in ORDER:
        a_y[d].wait_recv()
        pass_a(d)
    for d, copy in b_y:
        copy.wait_recv()
        from_y = (y + NY - d) % NY
        across.append(go(hid_b.at[from_y % YL, 0, from_y // YL], hid_b.at[from_y % YL, 1, from_y // YL], partner))
    for d, copy in c_z:
        copy.wait_recv()
        from_z = (z + NZ - d) % NZ
        across.append(go(hid_c.at[from_z, 0], hid_c.at[from_z, 1], partner))
    for d, dx, copy in a_x:
        copy.wait_recv()
        from_y, from_x = (y + NY - d) % NY, (x + NX - dx) % NX
        across.append(go(hid_a.at[from_y % YL, 0, from_y // YL, from_x],
                         hid_a.at[from_y % YL, 1, from_y // YL, from_x], partner))
    for copy in across:
        copy.wait_recv()
    for copy in fetch:
        copy.wait()

    def dot(a, b, dims):
        return lax.dot_general(a, b, (dims, ((), ())), preferred_element_type=F32)

    def rows_a(j):
        return hid_a[j].reshape(TALL, WA)

    def rows_b(j):
        return hid_b[j].reshape(TALL, WB)

    def rows_c(j):
        return hid_c[j].reshape(TALL, WC)

    def weight_a(j):
        return w_a[j].reshape(WA, VOCAB_DEV)

    def weight_b(j):
        return w_b[j].reshape(WB, VOCAB_DEV)

    def weight_c(j):
        return w_c[j].reshape(WC, VOCAB_DEV)

    nn, nt, tn = ((1,), (0,)), ((1,), (1,)), ((0,), (0,))
    logits = sum(dot(rows_a(j), weight_a(j), nn) + dot(rows_b(j), weight_b(j), nn) for j in range(YL))
    logits = logits + sum(dot(rows_c(j), weight_c(j), nn) for j in range(NZ))
    top = jnp.max(logits, axis=1, keepdims=True)
    shifted = jnp.exp(logits - top)
    total = jnp.sum(shifted, axis=1, keepdims=True)
    row = lax.broadcasted_iota(jnp.int32, (TALL, TOKENS), 0)
    section = (row // PAD) % NX * 4 + (row // (PAD * NX)) % YH * 2 + (row // HALF + c) % 2
    match = (section * ROWS + row % PAD == lax.broadcasted_iota(jnp.int32, (TALL, TOKENS), 1)) & (row % PAD < ROWS)
    goal = jnp.sum(jnp.where(match, targets[...].astype(F32), 0.0), axis=1, keepdims=True).astype(jnp.int32)
    vocab = lax.broadcasted_iota(jnp.int32, (TALL, VOCAB_DEV), 1) + (s * (YL * NZ) + t) * VOCAB_DEV
    hit = vocab == goal
    picked = jnp.sum(jnp.where(hit, logits, 0.0), axis=1, keepdims=True)

    lane = lax.broadcasted_iota(jnp.int32, (TALL, 128), 1)
    wide = jnp.where(lane == 0, top, jnp.where(lane == 1, total, jnp.where(lane == 2, picked, 0.0)))
    tall = wide.T[0:8, :]
    stat[0] = tall
    stat[3] = jnp.concatenate([tall[:, HALF:TALL], tall[:, 0:HALF]], axis=1)

    def merge(parts):
        best = functools.reduce(jnp.maximum, [p[0:1, :] for p in parts])
        amount = sum(p[1:2, :] * jnp.exp(p[0:1, :] - best) for p in parts)
        pick = sum(p[2:3, :] for p in parts)
        return jnp.concatenate([best, amount, pick, jnp.zeros((5, TALL), F32)], axis=0)

    def exchange(part, buf, sends):
        copies = [go(src, buf.at[i], peer) for i, (src, peer) in enumerate(sends)]
        for copy in copies:
            copy.wait_recv()
        return merge([part] + [buf[i] for i in range(len(sends))])

    part = exchange(tall, st_x, [(stat.at[3 if dc else 0], x_peer(d, dc)) for d, dc in xc])
    stat[1] = part
    part = exchange(part, st_y, [(stat.at[1], y_peer(d)) for d in ORDER])
    stat[2] = part
    part = exchange(part, st_z, [(stat.at[2], z_peer(d)) for d in ORDER])

    slot = lax.broadcasted_iota(jnp.int32, (1, TALL), 1)
    each = jnp.where(slot % PAD < ROWS, part[0:1, :] + jnp.log(part[1:2, :]) - part[2:3, :], 0.0)
    loss[0, 0] = jnp.sum(each) / TOKENS

    back = jnp.concatenate([part, jnp.zeros((120, TALL), F32)], axis=0).T
    ratio = shifted * jnp.exp(top - back[:, 0:1]) / back[:, 1:2]
    probs = ratio.astype(BF16)
    dlogits = (ratio - hit.astype(F32)).astype(BF16)

    def first_half(weight, keep, out, into):
        terms = dot(dlogits, weight, nt)
        shape = (YH, NX, PAD, terms.shape[1])
        keep[...] = terms[0:HALF].reshape(shape)
        out[...] = terms[HALF:TALL].astype(BF16).reshape(shape)
        return go(out, into, partner)

    turn = [(yl + k) % YL for k in range(YL)]
    core_a = [first_half(weight_a(turn[k]), keep_a.at[k], out_a.at[k], in_a.at[k]) for k in range(YL)]
    core_b = [first_half(weight_b(j), keep_b.at[j], out_b.at[j], in_b.at[j]) for j in range(YL)]
    core_c = [first_half(weight_c(j), keep_c.at[j], out_c.at[j], in_c.at[j]) for j in range(NZ)]

    def add_core(copy, keep, into, send):
        copy.wait_recv()
        both = keep[...] + into[...].astype(F32)
        keep[...] = both
        send[...] = both.astype(BF16)

    a_x = []
    for k in range(YL):
        add_core(core_a[k], keep_a.at[k], in_a.at[k], s1_a.at[k])
        a_x.append([go(s1_a.at[k, :, (x + d) % NX], r1_a.at[d, k], x_peer(d)) for d in XORDER])
    for j in range(YL):
        add_core(core_b[j], keep_b.at[j], in_b.at[j], s1_b.at[j])
    b_y = []
    for d in ORDER:
        to_y = (y + d) % NY
        b_y.append(go(s1_b.at[to_y % YL, to_y // YL], r1_b.at[d], y_peer(d)))
    for j in range(NZ):
        add_core(core_c[j], keep_c.at[j], in_c.at[j], s1_c.at[j])
    c_z = [go(s1_c.at[(z + d) % NZ], r1_c.at[d], z_peer(d)) for d in ORDER]

    for j in range(YL):
        g_a[j] = dot(rows_a(j), probs, tn).astype(BF16).reshape(NZ, FA, VOCAB_DEV)
        g_b[j] = dot(rows_b(j), probs, tn).astype(BF16).reshape(NZ, FB, VOCAB_DEV)
    for j in range(NZ):
        g_c[j] = dot(rows_c(j), probs, tn).astype(BF16).reshape(YL, FC, VOCAB_DEV)
    writes = [
        pltpu.make_async_copy(g_a, head_grad.at[:, :, 0:FA], gsem.at[0]),
        pltpu.make_async_copy(g_b, head_grad.at[:, :, FA:FA + FB], gsem.at[1]),
    ] + [
        pltpu.make_async_copy(g_c.at[i], head_grad.at[:, i, FA + FB:FEATS], gsem.at[2 + i]) for i in range(NZ)
    ]
    for write in writes:
        write.start()

    a_y = []
    for k in range(YL):
        for copy in a_x[k]:
            copy.wait_recv()
        chunk = keep_a[k, :, x] + sum(r1_a[d, k].astype(F32) for d in XORDER)
        s2_a[k] = chunk.astype(BF16)
        if k == 0:
            keep_a[0, :, 0] = chunk
        for e in range(YH):
            if k or e:
                to = (yh + e) % YH
                a_y.append(go(s2_a.at[k, to], r2_a.at[e * YL + k], at(x, to * YL + turn[k], z, c)))
    for copy in b_y:
        copy.wait_recv()
    sum_b = keep_b[yl, yh] + sum(r1_b[d].astype(F32) for d in ORDER)
    s2_b[...] = sum_b.astype(BF16)
    keep_b[0, 0] = sum_b
    b_x = [go(s2_b.at[(x + d) % NX], r2_b.at[d], x_peer(d)) for d in XORDER]
    for copy in c_z:
        copy.wait_recv()
    sum_c = keep_c[z] + sum(r1_c[d].astype(F32) for d in ORDER)
    s2_c[...] = sum_c.astype(BF16)
    keep_c[0] = sum_c
    c_x = [go(s2_c.at[:, (x + d) % NX], r2_c.at[d], x_peer(d)) for d in XORDER]

    for copy in c_x:
        copy.wait_recv()
    part_c = keep_c[0, :, x] + sum(r2_c[d].astype(F32) for d in XORDER)
    for i in range(NY):
        s3_c[i, :, 0:FC] = part_c[i // YL, :, FC * (i % YL):FC * (i % YL + 1)]
    c_y = [go(s3_c.at[(y + d) % NY], r3_c.at[d], y_peer(d)) for d in ORDER]
    for copy in b_x:
        copy.wait_recv()
    part_b = keep_b[0, 0, x] + sum(r2_b[d].astype(F32) for d in XORDER)
    for copy in a_y:
        copy.wait_recv()
    part_a = keep_a[0, yh, 0] + sum(r2_a[n].astype(F32) for n in range(1, NY))
    for i in range(NZ):
        s3_ab[i, :, 0:FA] = part_a[:, FA * i:FA * (i + 1)]
        s3_ab[i, :, FA:FA + FB] = part_b[:, FB * i:FB * (i + 1)]
    ab_z = [go(s3_ab.at[(z + d) % NZ], r3_ab.at[d], z_peer(d)) for d in ORDER]
    for copy in c_y:
        copy.wait_recv()
    done_c = s3_c[y][:, 0:FC] + sum(r3_c[d][:, 0:FC] for d in ORDER)
    hidden_grad[:, FA + FB:FEATS] = done_c[0:ROWS].astype(BF16)
    for copy in ab_z:
        copy.wait_recv()
    done_ab = s3_ab[z][:, 0:FA + FB] + sum(r3_ab[d][:, 0:FA + FB] for d in ORDER)
    hidden_grad[:, 0:FA + FB] = done_ab[0:ROWS].astype(BF16)

    for copy in sent:
        copy.wait_send()
    for write in writes:
        write.wait()


def per_device(hidden, head_weight, targets):
    vmem = pl.BlockSpec(memory_space=pltpu.VMEM)
    hbm = pl.BlockSpec(memory_space=pltpu.HBM)
    v = pltpu.VMEM
    dma = pltpu.SemaphoreType.DMA
    halves = (YH, NX, PAD)
    loss, head_grad, hidden_grad = pl.pallas_call(
        kernel,
        out_shape=(
            jax.ShapeDtypeStruct((1, 1), F32),
            jax.ShapeDtypeStruct((YL, NZ, FEATS, VOCAB_DEV), BF16),
            jax.ShapeDtypeStruct((ROWS, FEATS), BF16),
        ),
        in_specs=[hbm, hbm, hbm],
        out_specs=(pl.BlockSpec(memory_space=pltpu.SMEM), pl.BlockSpec(memory_space=pl.ANY), vmem),
        scratch_shapes=[
            v((ROWS, FEATS), BF16), v((1, TOKENS), jnp.int32),
            v((YL, NZ, FA, VOCAB_DEV), BF16), v((YL, NZ, FB, VOCAB_DEV), BF16), v((NZ, YL, FC, VOCAB_DEV), BF16),
            v((YL, NC) + halves + (WA,), BF16), v((YL, NC) + halves + (WB,), BF16), v((NZ, NC) + halves + (WC,), BF16),
            v((2, PAD, 128), F32), v((PAD, 128), BF16), v((PAD, 128), BF16),
            v((NZ, PAD, 128), BF16), v((NY, PAD, 128), BF16),
            v((PAD, WA), F32), v((PAD, WB), F32), v((YH, PAD, WC), F32),
            v((4, 8, TALL), F32), v((7, 8, TALL), F32), v((7, 8, TALL), F32), v((7, 8, TALL), F32),
            v((YL,) + halves + (WA,), F32), v((YL,) + halves + (WB,), F32), v((NZ,) + halves + (WC,), F32),
            v((YL,) + halves + (WA,), BF16), v((YL,) + halves + (WB,), BF16), v((NZ,) + halves + (WC,), BF16),
            v((YL,) + halves + (WA,), BF16), v((YL,) + halves + (WB,), BF16), v((NZ,) + halves + (WC,), BF16),
            v((YL,) + halves + (WA,), BF16), v((YL,) + halves + (WB,), BF16), v((NZ,) + halves + (WC,), BF16),
            v((NX, YL, YH, PAD, WA), BF16), v((NY, NX, PAD, WB), BF16), v((NZ,) + halves + (WC,), BF16),
            v((YL, YH, PAD, WA), BF16), v((NX, PAD, WB), BF16), v(halves + (WC,), BF16),
            v((NY, PAD, WA), BF16), v((NX, PAD, WB), BF16), v((NX, YH, PAD, WC), BF16),
            v((NZ, PAD, 128), F32), v((NY, PAD, 128), F32), v((NZ, PAD, 128), F32), v((NY, PAD, 128), F32),
            v((YL, NZ, FA, VOCAB_DEV), BF16), v((YL, NZ, FB, VOCAB_DEV), BF16), v((NZ, YL, FC, VOCAB_DEV), BF16),
            dma((12,)), dma((10,)), dma((208,)), dma((208,)),
        ],
        compiler_params=pltpu.CompilerParams(
            collective_id=0, has_side_effects=True, vmem_limit_bytes=44 * 2**20),
        name="output_layer",
    )(*[pltpu.with_memory_space_constraint(operand, pltpu.HBM) for operand in (
        hidden, head_weight.reshape(YL, NZ, FEATS, VOCAB_DEV), targets.reshape(1, TOKENS))])
    return loss.reshape(()), head_grad.reshape(D, VOCAB_DEV), hidden_grad


def solution(mesh):
    placed = (P("section", "tp"), P(None, ("section", "tp")), P())
    return jax.shard_map(
        per_device,
        mesh=mesh,
        in_specs=placed,
        out_specs=(P(), P(None, ("section", "tp")), P("section", "tp")),
        check_vma=False,
    )
```

time: 614 us -> 80.5 us (0.13)
  blocking collectives: 358 us -> 0 us
  waiting for transfers between devices: 216 us -> 0 us
  Pallas kernels: 0 us -> 75.6 us
  between operations: 16.5 us -> 2.33 us
  matrix products: 9.21 us -> 0 us
  local copies, waits for them, and re-layouts: 10.3 us -> 2.01 us
    reduce_scatter x1 -> x0, waiting for transfers between devices: 156 us -> none  [per_device(): lax.psum_scatter(whole_terms, 'tp', scatter_dimension=1, tiled=True)]
    pmax x1 -> x0, blocking collectives: 99.6 us -> none  [per_device(): top = lax.pmax(local_top, ('section', 'tp'))]
    psum x1 -> x0, blocking collectives: 94.8 us -> none  [per_device(): lax.psum((jnp.sum(shifted, axis=1), local_pick), ('section', 'tp'))]
    all_gather x1 -> x0, blocking collectives: 86.6 us -> none  [per_device(): columns = lax.all_gather(hidden, 'tp', axis=1, tiled=True)]
    unnamed x1 -> x0, blocking collectives: 76.7 us -> none
    pallas_call x0 -> x1, Pallas kernels: none -> 75.6 us  [per_device(): pl.pallas_call(kernel, out_shape=(jax.ShapeDtypeStruct((1, 1), F32), jax....]
    all_gather x1 -> x0, waiting for transfers between devices: 59.5 us -> none  [per_device(): full_states = lax.all_gather(columns, 'section', axis=0, tiled=True)]
    dot_general x3 -> x0, matrix products: 9.21 us -> none  [the longest x1 3.89 us: per_device(): lax.dot_general(full_states, probs, (((0,), (0,)), ((), ())), preferred_e...]
  transfers between devices with their start and end apart: 2 -> 0, of which waited for: 2 -> 0; matrix products, arithmetic and copies ran while one was open for 2% -> 0% of each run, Pallas kernels for 0% -> 0%
where the time goes in v2:
time: 80.5 us; the launch traced here: 80 us
  Pallas kernels  75.6 us (94%)
  between operations  2.33 us (3%)
  local copies, waits for them, and re-layouts  2.01 us (2%)
    pallas_call x1, Pallas kernels, per_device(): pl.pallas_call(kernel, out_shape=(jax.ShapeDtypeStruct((1, 1), F32), jax....  75.6 us
    unnamed x2, local copies, waits for them, and re-layouts  2.01 us

profile of v2, /device:TPU:6, one launch (start us, length us, event | category | flops | bytes accessed | tf_op | source)
XLA Modules:
  0.0 80.0 jit_solution(16150171025806482383)
XLA Ops:
  0.6 75.6 %output_layer.1 = (f32[1,1]{1,0:T(1,128)}, bf16[4,8,144,256]{3,2,1,0:T(8,128)(2,1)S(1)}, bf16[13,144]{1,0:T(8,128)(2,1)S(1)}) custom-call(bf16[13,144]{1,0:T(8,128)(2,1)} %shard_hbm.1, bf16[4,8,144,256]{3,2,1,0:T(8,128)(2,1)} %bitcast.5, s32[1,208]{1,0:T(1,128)} %bitcast.6), custom_call_target="tpu_custom_call" | custom-call | tf_op jit(solution)/shard_map/output_layer/pallas_call | solution.py:336
  76.8 1.4 %copy.10 = bf16[4608,256]{1,0:T(8,128)(2,1)} copy(bf16[4608,256]{1,0:T(8,128)(2,1)S(1)} %bitcast.4) | data formatting | bytes 4718592
  78.2 0.6 copy.11

commit v3 on v2

--- a/solution.py
+++ b/solution.py
@@ -24,14 +24,15 @@
 TOKENS = 208
 ORDER = (1, 7, 2, 6, 3, 5, 4)
 XORDER = (1, 3, 2)
+MISS = 2 * len(ORDER) + 1
 
 
 def kernel(shard_hbm, weight_hbm, targets_hbm, loss, head_grad, hidden_grad,
-           shard, targets, w_a, w_b, w_c, hid_a, hid_b, hid_c, pad32, own_ab, own_c, z_rec, y_rec,
-           line_a, line_b, line_c, stat, st_x, st_y, st_z,
-           keep_a, keep_b, keep_c, out_a, out_b, out_c, in_a, in_b, in_c,
-           s1_a, s1_b, s1_c, r1_a, r1_b, r1_c, s2_a, s2_b, s2_c, r2_a, r2_b, r2_c,
-           s3_ab, s3_c, r3_ab, r3_c, g_a, g_b, g_c, local, gsem, ssem, rsem):
+           shard, targets, w_a, w_b, w_c, wt_a, wt_b, wt_c, hid_a, hid_b, hid_c, pad32, own_ab, own_c,
+           z_rec, y_rec, line_a, line_b, line_c, stat, st_x, st_y, st_m, st_z, coef, keep_a, keep_b, keep_c,
+           out_a, out_b, out_c, in_a, in_b, in_c, s1_a, s1_b, s1_c, r1_a, r1_b, r1_c, tk_a, tk_b, tk_c,
+           to_a, to_b, to_c, ti_a, ti_b, ti_c, tr_a, tr_b, tr_c, s2_a, s2_b, s2_c, r2_a, r2_b, r2_c, s3_ab,
+           s3_c, r3_ab, r3_c, g_a, g_b, g_c, local, gsem, ssem, rsem):
     s = lax.axis_index("section")
     t = lax.axis_index("tp")
     x, yh, c = s // 4, (s // 2) % 2, s % 2
@@ -59,6 +60,13 @@
         copy.start()
         sent.append(copy)
         return copy
+
+    xc = [(d, dc) for d in range(NX) for dc in range(NC) if d or dc]
+    peers = [z_peer(d) for d in ORDER] + [y_peer(d) for d in ORDER] + [x_peer(d, dc) for d, dc in xc]
+    partner = x_peer(0, 1)
+    barrier = pltpu.get_barrier_semaphore()
+    for peer in peers:
+        pl.semaphore_signal(barrier, inc=1, device_id=peer, device_id_type=MESH)
 
     fetch_small = [
         pltpu.make_async_copy(shard_hbm, shard, local.at[0]),
@@ -73,12 +81,6 @@
     for copy in fetch_small + fetch:
         copy.start()
 
-    xc = [(d, dc) for d in range(NX) for dc in range(NC) if d or dc]
-    peers = [z_peer(d) for d in ORDER] + [y_peer(d) for d in ORDER] + [x_peer(d, dc) for d, dc in xc]
-    barrier = pltpu.get_barrier_semaphore()
-    for peer in peers:
-        pl.semaphore_signal(barrier, inc=1, device_id=peer, device_id_type=MESH)
-
     for copy in fetch_small:
         copy.wait()
     pad32[...] = jnp.zeros_like(pad32)
@@ -87,12 +89,50 @@
     mine_ab, mine_c = pad32[0].astype(BF16), pad32[1].astype(BF16)
     own_ab[...] = mine_ab
     own_c[...] = mine_c
+
+    row = lax.broadcasted_iota(jnp.int32, (TALL, TOKENS), 0)
+    section = (row // PAD) % NX * 4 + (row // (PAD * NX)) % YH * 2 + (row // HALF + c) % 2
+    match = (section * ROWS + row % PAD == lax.broadcasted_iota(jnp.int32, (TALL, TOKENS), 1)) & (row % PAD < ROWS)
+    goal = jnp.sum(jnp.where(match, targets[...].astype(F32), 0.0), axis=1, keepdims=True).astype(jnp.int32)
+    vocab = lax.broadcasted_iota(jnp.int32, (TALL, VOCAB_DEV), 1) + (s * (YL * NZ) + t) * VOCAB_DEV
+    hit = vocab == goal
+
+    def dot(a, b, dims):
+        return lax.dot_general(a, b, (dims, ((), ())), preferred_element_type=F32)
+
+    nn, tn = ((1,), (0,)), ((0,), (0,))
+    turn = [(yl + k) % YL for k in range(YL)]
+
+    for copy in fetch:
+        copy.wait()
+    for j in range(YL):
+        wt_a[j] = w_a[j].reshape(WA, VOCAB_DEV).T
+        wt_b[j] = w_b[j].reshape(WB, VOCAB_DEV).T
+    for j in range(NZ):
+        wt_c[j] = w_c[j].reshape(WC, VOCAB_DEV).T
+
+    def split(left, weight, keep, out):
+        terms = dot(left, weight, nn)
+        shape = (YH, NX, PAD, terms.shape[1])
+        keep[...] = terms[0:HALF].astype(keep.dtype).reshape(shape)
+        out[...] = terms[HALF:TALL].astype(BF16).reshape(shape)
+
+    hot = hit.astype(F32).astype(BF16)
+    for k in range(YL):
+        split(hot, wt_a[turn[k]], tk_a.at[k], to_a.at[k])
+    for j in range(YL):
+        split(hot, wt_b[j], tk_b.at[j], to_b.at[j])
+    for j in range(NZ):
+        split(hot, wt_c[j], tk_c.at[j], to_c.at[j])
     pl.semaphore_wait(barrier, len(peers))
 
     z_copies = [go(own_ab, z_rec.at[z], z_peer(d)) for d in ORDER]
     y_copies = [go(own_c, y_rec.at[y], y_peer(d)) for d in ORDER]
     z_rec[z] = mine_ab
     y_rec[y] = mine_c
+    t_core = [go(to_a.at[k], ti_a.at[k], partner) for k in range(YL)]
+    t_core += [go(to_b.at[j], ti_b.at[j], partner) for j in range(YL)]
+    t_core += [go(to_c.at[j], ti_c.at[j], partner) for j in range(NZ)]
     for copy in z_copies:
         copy.wait_recv()
     for i in range(NZ):
@@ -102,11 +142,15 @@
     hid_a[yl, 0, yh, x] = line_a[...].astype(BF16)
     hid_b[yl, 0, yh, x] = line_b[...].astype(BF16)
 
-    partner = x_peer(0, 1)
     block = hid_a.at[yl, 0, yh, x]
     a_y = {d: go(block, block, y_peer(d)) for d in ORDER}
     block = hid_b.at[yl, 0, yh, x]
     b_x = [go(block, block, x_peer(d)) for d in XORDER]
+    for copy in t_core:
+        copy.wait_recv()
+    for keep, into in ((tk_a, ti_a), (tk_b, ti_b), (tk_c, ti_c)):
+        for j in range(keep.shape[0]):
+            keep[j] = keep[j] + into[j]
     for copy in y_copies:
         copy.wait_recv()
     for i in range(NY):
@@ -152,13 +196,20 @@
         from_y, from_x = (y + NY - d) % NY, (x + NX - dx) % NX
         across.append(go(hid_a.at[from_y % YL, 0, from_y // YL, from_x],
                          hid_a.at[from_y % YL, 1, from_y // YL, from_x], partner))
+    def wide_a(src, dst, k):
+        return [go(src.at[k, :, (x + d) % NX], dst.at[d, k], x_peer(d)) for d in XORDER]
+
+    def wide_b(src, dst):
+        return [go(src.at[(y + d) % NY % YL, (y + d) % NY // YL], dst.at[d], y_peer(d)) for d in ORDER]
+
+    def wide_c(src, dst):
+        return [go(src.at[(z + d) % NZ], dst.at[d], z_peer(d)) for d in ORDER]
+
+    ta_x = [wide_a(tk_a, tr_a, k) for k in range(YL)]
+    tb_y = wide_b(tk_b, tr_b)
+    tc_z = wide_c(tk_c, tr_c)
     for copy in across:
         copy.wait_recv()
-    for copy in fetch:
-        copy.wait()
-
-    def dot(a, b, dims):
-        return lax.dot_general(a, b, (dims, ((), ())), preferred_element_type=F32)
 
     def rows_a(j):
         return hid_a[j].reshape(TALL, WA)
@@ -169,73 +220,54 @@
     def rows_c(j):
         return hid_c[j].reshape(TALL, WC)
 
-    def weight_a(j):
-        return w_a[j].reshape(WA, VOCAB_DEV)
-
-    def weight_b(j):
-        return w_b[j].reshape(WB, VOCAB_DEV)
-
-    def weight_c(j):
-        return w_c[j].reshape(WC, VOCAB_DEV)
-
-    nn, nt, tn = ((1,), (0,)), ((1,), (1,)), ((0,), (0,))
-    logits = sum(dot(rows_a(j), weight_a(j), nn) + dot(rows_b(j), weight_b(j), nn) for j in range(YL))
-    logits = logits + sum(dot(rows_c(j), weight_c(j), nn) for j in range(NZ))
+    logits = sum(dot(rows_a(j), w_a[j].reshape(WA, VOCAB_DEV), nn) + dot(rows_b(j), w_b[j].reshape(WB, VOCAB_DEV), nn)
+                 for j in range(YL))
+    logits = logits + sum(dot(rows_c(j), w_c[j].reshape(WC, VOCAB_DEV), nn) for j in range(NZ))
     top = jnp.max(logits, axis=1, keepdims=True)
     shifted = jnp.exp(logits - top)
-    total = jnp.sum(shifted, axis=1, keepdims=True)
-    row = lax.broadcasted_iota(jnp.int32, (TALL, TOKENS), 0)
-    section = (row // PAD) % NX * 4 + (row // (PAD * NX)) % YH * 2 + (row // HALF + c) % 2
-    match = (section * ROWS + row % PAD == lax.broadcasted_iota(jnp.int32, (TALL, TOKENS), 1)) & (row % PAD < ROWS)
-    goal = jnp.sum(jnp.where(match, targets[...].astype(F32), 0.0), axis=1, keepdims=True).astype(jnp.int32)
-    vocab = lax.broadcasted_iota(jnp.int32, (TALL, VOCAB_DEV), 1) + (s * (YL * NZ) + t) * VOCAB_DEV
-    hit = vocab == goal
+    rest = jnp.sum(jnp.where(hit, 0.0, shifted), axis=1, keepdims=True)
+    aim = jnp.sum(jnp.where(hit, shifted, 0.0), axis=1, keepdims=True)
     picked = jnp.sum(jnp.where(hit, logits, 0.0), axis=1, keepdims=True)
 
     lane = lax.broadcasted_iota(jnp.int32, (TALL, 128), 1)
-    wide = jnp.where(lane == 0, top, jnp.where(lane == 1, total, jnp.where(lane == 2, picked, 0.0)))
-    tall = wide.T[0:8, :]
+    columns = jnp.where(lane == 0, top, jnp.where(lane == 1, rest, jnp.where(lane == 2, picked, jnp.where(
+        lane == 3, aim, 0.0))))
+    tall = columns.T[0:8, :]
     stat[0] = tall
     stat[3] = jnp.concatenate([tall[:, HALF:TALL], tall[:, 0:HALF]], axis=1)
 
     def merge(parts):
         best = functools.reduce(jnp.maximum, [p[0:1, :] for p in parts])
-        amount = sum(p[1:2, :] * jnp.exp(p[0:1, :] - best) for p in parts)
-        pick = sum(p[2:3, :] for p in parts)
-        return jnp.concatenate([best, amount, pick, jnp.zeros((5, TALL), F32)], axis=0)
-
-    def exchange(part, buf, sends):
-        copies = [go(src, buf.at[i], peer) for i, (src, peer) in enumerate(sends)]
-        for copy in copies:
-            copy.wait_recv()
-        return merge([part] + [buf[i] for i in range(len(sends))])
-
-    part = exchange(tall, st_x, [(stat.at[3 if dc else 0], x_peer(d, dc)) for d, dc in xc])
-    stat[1] = part
-    part = exchange(part, st_y, [(stat.at[1], y_peer(d)) for d in ORDER])
-    stat[2] = part
-    part = exchange(part, st_z, [(stat.at[2], z_peer(d)) for d in ORDER])
-
-    slot = lax.broadcasted_iota(jnp.int32, (1, TALL), 1)
-    each = jnp.where(slot % PAD < ROWS, part[0:1, :] + jnp.log(part[1:2, :]) - part[2:3, :], 0.0)
-    loss[0, 0] = jnp.sum(each) / TOKENS
-
-    back = jnp.concatenate([part, jnp.zeros((120, TALL), F32)], axis=0).T
-    ratio = shifted * jnp.exp(top - back[:, 0:1]) / back[:, 1:2]
-    probs = ratio.astype(BF16)
-    dlogits = (ratio - hit.astype(F32)).astype(BF16)
-
-    def first_half(weight, keep, out, into):
-        terms = dot(dlogits, weight, nt)
-        shape = (YH, NX, PAD, terms.shape[1])
-        keep[...] = terms[0:HALF].reshape(shape)
-        out[...] = terms[HALF:TALL].astype(BF16).reshape(shape)
-        return go(out, into, partner)
-
-    turn = [(yl + k) % YL for k in range(YL)]
-    core_a = [first_half(weight_a(turn[k]), keep_a.at[k], out_a.at[k], in_a.at[k]) for k in range(YL)]
-    core_b = [first_half(weight_b(j), keep_b.at[j], out_b.at[j], in_b.at[j]) for j in range(YL)]
-    core_c = [first_half(weight_c(j), keep_c.at[j], out_c.at[j], in_c.at[j]) for j in range(NZ)]
+        scale = [jnp.exp(p[0:1, :] - best) for p in parts]
+        rest_ = sum(p[1:2, :] * f for p, f in zip(parts, scale))
+        pick_ = sum(p[2:3, :] for p in parts)
+        aim_ = sum(p[3:4, :] * f for p, f in zip(parts, scale))
+        return jnp.concatenate([best, rest_, pick_, aim_, jnp.zeros((4, TALL), F32)], axis=0)
+
+    def columns_of(rows):
+        full = jnp.concatenate(rows + [jnp.zeros((128 - len(rows), TALL), F32)], axis=0)
+        return full.T
+
+    copies = [go(stat.at[3 if dc else 0], st_x.at[i], x_peer(d, dc)) for i, (d, dc) in enumerate(xc)]
+    for copy in copies:
+        copy.wait_recv()
+    group = merge([tall] + [st_x[i] for i in range(len(xc))])
+    stat[1] = group
+    to_y = [go(stat.at[1], st_y.at[i], y_peer(d)) for i, d in enumerate(ORDER)]
+    to_z = [go(stat.at[1], st_m.at[i], z_peer(d)) for i, d in enumerate(ORDER)]
+
+    shifted = jnp.exp(logits - columns_of([group])[:, 0:1])
+    others = jnp.where(hit, 0.0, shifted).astype(BF16)
+    core_a, core_b, core_c = [], [], []
+    for k in range(YL):
+        split(others, wt_a[turn[k]], keep_a.at[k], out_a.at[k])
+        core_a.append(go(out_a.at[k], in_a.at[k], partner))
+    for j in range(YL):
+        split(others, wt_b[j], keep_b.at[j], out_b.at[j])
+        core_b.append(go(out_b.at[j], in_b.at[j], partner))
+    for j in range(NZ):
+        split(others, wt_c[j], keep_c.at[j], out_c.at[j])
+        core_c.append(go(out_c.at[j], in_c.at[j], partner))
 
     def add_core(copy, keep, into, send):
         copy.wait_recv()
@@ -246,16 +278,70 @@
     a_x = []
     for k in range(YL):
         add_core(core_a[k], keep_a.at[k], in_a.at[k], s1_a.at[k])
-        a_x.append([go(s1_a.at[k, :, (x + d) % NX], r1_a.at[d, k], x_peer(d)) for d in XORDER])
+        a_x.append(wide_a(s1_a, r1_a, k))
+    for copy in to_y:
+        copy.wait_recv()
+    near = [st_y[i] for i in range(len(ORDER))]
+    plane = merge([group] + near)
+    stat[2] = plane
+    last = [go(stat.at[2], st_z.at[i], z_peer(d)) for i, d in enumerate(ORDER)]
     for j in range(YL):
         add_core(core_b[j], keep_b.at[j], in_b.at[j], s1_b.at[j])
-    b_y = []
-    for d in ORDER:
-        to_y = (y + d) % NY
-        b_y.append(go(s1_b.at[to_y % YL, to_y // YL], r1_b.at[d], y_peer(d)))
+    b_y = wide_b(s1_b, r1_b)
     for j in range(NZ):
         add_core(core_c[j], keep_c.at[j], in_c.at[j], s1_c.at[j])
-    c_z = [go(s1_c.at[(z + d) % NZ], r1_c.at[d], z_peer(d)) for d in ORDER]
+    c_z = wide_c(s1_c, r1_c)
+
+    for copy in to_z + last:
+        copy.wait_recv()
+    whole = merge([plane] + [st_z[i] for i in range(len(ORDER))])
+    highest, total = whole[0:1, :], whole[1:2, :] + whole[3:4, :]
+    slot = lax.broadcasted_iota(jnp.int32, (1, TALL), 1)
+    each = jnp.where(slot % PAD < ROWS, highest + jnp.log(total) - whole[2:3, :], 0.0)
+    loss[0, 0] = jnp.sum(each) / TOKENS
+
+    def factor(p):
+        return jnp.exp(p[0:1, :] - highest) / total
+
+    miss = (whole[1:2, :] / total).astype(BF16).astype(F32)
+    factors = columns_of([factor(group)] + [factor(p) for p in near]
+                         + [factor(st_m[i]) for i in range(len(ORDER))] + [miss])
+    coef[...] = factors[0:HALF].reshape(YH, NX, PAD, 128)
+    probs = (shifted * factors[:, 0:1]).astype(BF16)
+
+    a_y = []
+    f_x = coef[:, x]
+    for k in range(YL):
+        for copy in a_x[k] + ta_x[k]:
+            copy.wait_recv()
+        chunk = keep_a[k, :, x] + sum(r1_a[d, k].astype(F32) for d in XORDER)
+        column = tk_a[k, :, x] + sum(tr_a[d, k] for d in XORDER)
+        chunk = chunk * f_x[..., 0:1] - column.astype(F32) * f_x[..., MISS:MISS + 1]
+        s2_a[k] = chunk.astype(BF16)
+        if k == 0:
+            keep_a[0, :, 0] = chunk
+        for e in range(YH):
+            if k or e:
+                to = (yh + e) % YH
+                a_y.append(go(s2_a.at[k, to], r2_a.at[e * YL + k], at(x, to * YL + turn[k], z, c)))
+    for copy in b_y + tb_y:
+        copy.wait_recv()
+    f_y = coef[yh]
+    column = tk_b[yl, yh] + sum(tr_b[d] for d in ORDER)
+    sum_b = keep_b[yl, yh] * f_y[..., 0:1] - column.astype(F32) * f_y[..., MISS:MISS + 1]
+    sum_b = sum_b + sum(r1_b[d].astype(F32) * f_y[..., 1 + i:2 + i] for i, d in enumerate(ORDER))
+    s2_b[...] = sum_b.astype(BF16)
+    keep_b[0, 0] = sum_b
+    b_x = [go(s2_b.at[(x + d) % NX], r2_b.at[d], x_peer(d)) for d in XORDER]
+    for copy in c_z + tc_z:
+        copy.wait_recv()
+    f_z = coef[...]
+    column = tk_c[z] + sum(tr_c[d] for d in ORDER)
+    sum_c = keep_c[z] * f_z[..., 0:1] - column.astype(F32) * f_z[..., MISS:MISS + 1]
+    sum_c = sum_c + sum(r1_c[d].astype(F32) * f_z[..., 8 + i:9 + i] for i, d in enumerate(ORDER))
+    s2_c[...] = sum_c.astype(BF16)
+    keep_c[0] = sum_c
+    c_x = [go(s2_c.at[:, (x + d) % NX], r2_c.at[d], x_peer(d)) for d in XORDER]
 
     for j in range(YL):
         g_a[j] = dot(rows_a(j), probs, tn).astype(BF16).reshape(NZ, FA, VOCAB_DEV)
@@ -270,31 +356,6 @@
     ]
     for write in writes:
         write.start()
-
-    a_y = []
-    for k in range(YL):
-        for copy in a_x[k]:
-            copy.wait_recv()
-        chunk = keep_a[k, :, x] + sum(r1_a[d, k].astype(F32) for d in XORDER)
-        s2_a[k] = chunk.astype(BF16)
-        if k == 0:
-            keep_a[0, :, 0] = chunk
-        for e in range(YH):
-            if k or e:
-                to = (yh + e) % YH
-                a_y.append(go(s2_a.at[k, to], r2_a.at[e * YL + k], at(x, to * YL + turn[k], z, c)))
-    for copy in b_y:
-        copy.wait_recv()
-    sum_b = keep_b[yl, yh] + sum(r1_b[d].astype(F32) for d in ORDER)
-    s2_b[...] = sum_b.astype(BF16)
-    keep_b[0, 0] = sum_b
-    b_x = [go(s2_b.at[(x + d) % NX], r2_b.at[d], x_peer(d)) for d in XORDER]
-    for copy in c_z:
-        copy.wait_recv()
-    sum_c = keep_c[z] + sum(r1_c[d].astype(F32) for d in ORDER)
-    s2_c[...] = sum_c.astype(BF16)
-    keep_c[0] = sum_c
-    c_x = [go(s2_c.at[:, (x + d) % NX], r2_c.at[d], x_peer(d)) for d in XORDER]
 
     for copy in c_x:
         copy.wait_recv()
@@ -345,12 +406,18 @@
         scratch_shapes=[
             v((ROWS, FEATS), BF16), v((1, TOKENS), jnp.int32),
             v((YL, NZ, FA, VOCAB_DEV), BF16), v((YL, NZ, FB, VOCAB_DEV), BF16), v((NZ, YL, FC, VOCAB_DEV), BF16),
+            v((YL, VOCAB_DEV, WA), BF16), v((YL, VOCAB_DEV, WB), BF16), v((NZ, VOCAB_DEV, WC), BF16),
             v((YL, NC) + halves + (WA,), BF16), v((YL, NC) + halves + (WB,), BF16), v((NZ, NC) + halves + (WC,), BF16),
             v((2, PAD, 128), F32), v((PAD, 128), BF16), v((PAD, 128), BF16),
             v((NZ, PAD, 128), BF16), v((NY, PAD, 128), BF16),
             v((PAD, WA), F32), v((PAD, WB), F32), v((YH, PAD, WC), F32),
-            v((4, 8, TALL), F32), v((7, 8, TALL), F32), v((7, 8, TALL), F32), v((7, 8, TALL), F32),
+            v((4, 8, TALL), F32), v((7, 8, TALL), F32), v((7, 8, TALL), F32), v((7, 8, TALL), F32), v((7, 8, TALL), F32),
+            v(halves + (128,), F32),
             v((YL,) + halves + (WA,), F32), v((YL,) + halves + (WB,), F32), v((NZ,) + halves + (WC,), F32),
+            v((YL,) + halves + (WA,), BF16), v((YL,) + halves + (WB,), BF16), v((NZ,) + halves + (WC,), BF16),
+            v((YL,) + halves + (WA,), BF16), v((YL,) + halves + (WB,), BF16), v((NZ,) + halves + (WC,), BF16),
+            v((YL,) + halves + (WA,), BF16), v((YL,) + halves + (WB,), BF16), v((NZ,) + halves + (WC,), BF16),
+            v((NX, YL, YH, PAD, WA), BF16), v((NY, NX, PAD, WB), BF16), v((NZ,) + halves + (WC,), BF16),
             v((YL,) + halves + (WA,), BF16), v((YL,) + halves + (WB,), BF16), v((NZ,) + halves + (WC,), BF16),
             v((YL,) + halves + (WA,), BF16), v((YL,) + halves + (WB,), BF16), v((NZ,) + halves + (WC,), BF16),
             v((YL,) + halves + (WA,), BF16), v((YL,) + halves + (WB,), BF16), v((NZ,) + halves + (WC,), BF16),
@@ -359,7 +426,7 @@
             v((NY, PAD, WA), BF16), v((NX, PAD, WB), BF16), v((NX, YH, PAD, WC), BF16),
             v((NZ, PAD, 128), F32), v((NY, PAD, 128), F32), v((NZ, PAD, 128), F32), v((NY, PAD, 128), F32),
             v((YL, NZ, FA, VOCAB_DEV), BF16), v((YL, NZ, FB, VOCAB_DEV), BF16), v((NZ, YL, FC, VOCAB_DEV), BF16),
-            dma((12,)), dma((10,)), dma((208,)), dma((208,)),
+            dma((12,)), dma((10,)), dma((256,)), dma((256,)),
         ],
         compiler_params=pltpu.CompilerParams(
             collective_id=0, has_side_effects=True, vmem_limit_bytes=44 * 2**20),

time: 80.5 us -> 75.1 us (0.933)
  the two profiles are of different devices: /device:TPU:6 before, /device:TPU:8 now
where the time goes in v3:
time: 75.1 us; the launch traced here: 74.9 us
  Pallas kernels  70.6 us (94%)
  between operations  2.33 us (3%)
  local copies, waits for them, and re-layouts  2.01 us (3%)
    pallas_call x1, Pallas kernels, per_device(): pl.pallas_call(kernel, out_shape=(jax.ShapeDtypeStruct((1, 1), F32), jax....  70.6 us
    unnamed x2, local copies, waits for them, and re-layouts  2.01 us

profile of v3, /device:TPU:8, one launch (start us, length us, event | category | flops | bytes accessed | tf_op | source)
XLA Modules:
  0.0 74.9 jit_solution(2669072155154833974)
XLA Ops:
  0.6 70.6 %output_layer.1 = (f32[1,1]{1,0:T(1,128)}, bf16[4,8,144,256]{3,2,1,0:T(8,128)(2,1)S(1)}, bf16[13,144]{1,0:T(8,128)(2,1)S(1)}) custom-call(bf16[13,144]{1,0:T(8,128)(2,1)} %shard_hbm.1, bf16[4,8,144,256]{3,2,1,0:T(8,128)(2,1)} %bitcast.5, s32[1,208]{1,0:T(1,128)} %bitcast.6), custom_call_target="tpu_custom_call" | custom-call | tf_op jit(solution)/shard_map/output_layer/pallas_call | solution.py:397
  71.8 1.4 %copy.10 = bf16[4608,256]{1,0:T(8,128)(2,1)} copy(bf16[4608,256]{1,0:T(8,128)(2,1)S(1)} %bitcast.4) | data formatting | bytes 4718592
  73.2 0.6 copy.11

commit v4 on v3

--- a/solution.py
+++ b/solution.py
@@ -24,12 +24,13 @@
 TOKENS = 208
 ORDER = (1, 7, 2, 6, 3, 5, 4)
 XORDER = (1, 3, 2)
-MISS = 2 * len(ORDER) + 1
+FROM_X, FROM_Y, FROM_Z = 1, 4, 11
+MISS = 18
 
 
 def kernel(shard_hbm, weight_hbm, targets_hbm, loss, head_grad, hidden_grad,
            shard, targets, w_a, w_b, w_c, wt_a, wt_b, wt_c, hid_a, hid_b, hid_c, pad32, own_ab, own_c,
-           z_rec, y_rec, line_a, line_b, line_c, stat, st_x, st_y, st_m, st_z, coef, keep_a, keep_b, keep_c,
+           z_rec, y_rec, line_a, line_b, line_c, stat, st_c, st_x, st_y, st_m, st_n, st_z, coef, keep_a, keep_b, keep_c,
            out_a, out_b, out_c, in_a, in_b, in_c, s1_a, s1_b, s1_c, r1_a, r1_b, r1_c, tk_a, tk_b, tk_c,
            to_a, to_b, to_c, ti_a, ti_b, ti_c, tr_a, tr_b, tr_c, s2_a, s2_b, s2_c, r2_a, r2_b, r2_c, s3_ab,
            s3_c, r3_ab, r3_c, g_a, g_b, g_c, local, gsem, ssem, rsem):
@@ -48,8 +49,8 @@
     def y_peer(d):
         return at(x, (y + d) % NY, z, c)
 
-    def x_peer(d, dc=0):
-        return at((x + d) % NX, y, z, (c + dc) % 2)
+    def x_peer(d):
+        return at((x + d) % NX, y, z, c)
 
     sent = []
 
@@ -61,9 +62,9 @@
         sent.append(copy)
         return copy
 
-    xc = [(d, dc) for d in range(NX) for dc in range(NC) if d or dc]
-    peers = [z_peer(d) for d in ORDER] + [y_peer(d) for d in ORDER] + [x_peer(d, dc) for d, dc in xc]
-    partner = x_peer(0, 1)
+    peers = [z_peer(d) for d in ORDER] + [y_peer(d) for d in ORDER] + [x_peer(d) for d in XORDER]
+    partner = at(x, y, z, 1 - c)
+    peers.append(partner)
     barrier = pltpu.get_barrier_semaphore()
     for peer in peers:
         pl.semaphore_signal(barrier, inc=1, device_id=peer, device_id_type=MESH)
@@ -103,6 +104,13 @@
     nn, tn = ((1,), (0,)), ((0,), (0,))
     turn = [(yl + k) % YL for k in range(YL)]
 
+    pl.semaphore_wait(barrier, len(peers))
+
+    z_copies = [go(own_ab, z_rec.at[z], z_peer(d)) for d in ORDER]
+    y_copies = [go(own_c, y_rec.at[y], y_peer(d)) for d in ORDER]
+    z_rec[z] = mine_ab
+    y_rec[y] = mine_c
+
     for copy in fetch:
         copy.wait()
     for j in range(YL):
@@ -118,21 +126,17 @@
         out[...] = terms[HALF:TALL].astype(BF16).reshape(shape)
 
     hot = hit.astype(F32).astype(BF16)
+    t_core = []
     for k in range(YL):
         split(hot, wt_a[turn[k]], tk_a.at[k], to_a.at[k])
+        t_core.append(go(to_a.at[k], ti_a.at[k], partner))
     for j in range(YL):
         split(hot, wt_b[j], tk_b.at[j], to_b.at[j])
+        t_core.append(go(to_b.at[j], ti_b.at[j], partner))
     for j in range(NZ):
         split(hot, wt_c[j], tk_c.at[j], to_c.at[j])
-    pl.semaphore_wait(barrier, len(peers))
-
-    z_copies = [go(own_ab, z_rec.at[z], z_peer(d)) for d in ORDER]
-    y_copies = [go(own_c, y_rec.at[y], y_peer(d)) for d in ORDER]
-    z_rec[z] = mine_ab
-    y_rec[y] = mine_c
-    t_core = [go(to_a.at[k], ti_a.at[k], partner) for k in range(YL)]
-    t_core += [go(to_b.at[j], ti_b.at[j], partner) for j in range(YL)]
-    t_core += [go(to_c.at[j], ti_c.at[j], partner) for j in range(NZ)]
+        t_core.append(go(to_c.at[j], ti_c.at[j], partner))
+
     for copy in z_copies:
         copy.wait_recv()
     for i in range(NZ):
@@ -146,11 +150,6 @@
     a_y = {d: go(block, block, y_peer(d)) for d in ORDER}
     block = hid_b.at[yl, 0, yh, x]
     b_x = [go(block, block, x_peer(d)) for d in XORDER]
-    for copy in t_core:
-        copy.wait_recv()
-    for keep, into in ((tk_a, ti_a), (tk_b, ti_b), (tk_c, ti_c)):
-        for j in range(keep.shape[0]):
-            keep[j] = keep[j] + into[j]
     for copy in y_copies:
         copy.wait_recv()
     for i in range(NY):
@@ -183,6 +182,23 @@
     for d in ORDER:
         a_y[d].wait_recv()
         pass_a(d)
+
+    def wide_a(src, dst, k):
+        return [go(src.at[k, :, (x + d) % NX], dst.at[d, k], x_peer(d)) for d in XORDER]
+
+    def wide_b(src, dst):
+        return [go(src.at[(y + d) % NY % YL, (y + d) % NY // YL], dst.at[d], y_peer(d)) for d in ORDER]
+
+    def wide_c(src, dst):
+        return [go(src.at[(z + d) % NZ], dst.at[d], z_peer(d)) for d in ORDER]
+
+    for copy in t_core:
+        copy.wait_recv()
+    for keep, into in ((tk_a, ti_a), (tk_b, ti_b), (tk_c, ti_c)):
+        for j in range(keep.shape[0]):
+            keep[j] = keep[j] + into[j]
+    ta_x = [wide_a(tk_a, tr_a, k) for k in range(YL)]
+
     for d, copy in b_y:
         copy.wait_recv()
         from_y = (y + NY - d) % NY
@@ -196,16 +212,6 @@
         from_y, from_x = (y + NY - d) % NY, (x + NX - dx) % NX
         across.append(go(hid_a.at[from_y % YL, 0, from_y // YL, from_x],
                          hid_a.at[from_y % YL, 1, from_y // YL, from_x], partner))
-    def wide_a(src, dst, k):
-        return [go(src.at[k, :, (x + d) % NX], dst.at[d, k], x_peer(d)) for d in XORDER]
-
-    def wide_b(src, dst):
-        return [go(src.at[(y + d) % NY % YL, (y + d) % NY // YL], dst.at[d], y_peer(d)) for d in ORDER]
-
-    def wide_c(src, dst):
-        return [go(src.at[(z + d) % NZ], dst.at[d], z_peer(d)) for d in ORDER]
-
-    ta_x = [wide_a(tk_a, tr_a, k) for k in range(YL)]
     tb_y = wide_b(tk_b, tr_b)
     tc_z = wide_c(tk_c, tr_c)
     for copy in across:
@@ -248,43 +254,46 @@
         full = jnp.concatenate(rows + [jnp.zeros((128 - len(rows), TALL), F32)], axis=0)
         return full.T
 
-    copies = [go(stat.at[3 if dc else 0], st_x.at[i], x_peer(d, dc)) for i, (d, dc) in enumerate(xc)]
-    for copy in copies:
-        copy.wait_recv()
-    group = merge([tall] + [st_x[i] for i in range(len(xc))])
-    stat[1] = group
-    to_y = [go(stat.at[1], st_y.at[i], y_peer(d)) for i, d in enumerate(ORDER)]
-    to_z = [go(stat.at[1], st_m.at[i], z_peer(d)) for i, d in enumerate(ORDER)]
-
-    shifted = jnp.exp(logits - columns_of([group])[:, 0:1])
+    mate = go(stat.at[3], st_c, partner)
+
     others = jnp.where(hit, 0.0, shifted).astype(BF16)
     core_a, core_b, core_c = [], [], []
     for k in range(YL):
         split(others, wt_a[turn[k]], keep_a.at[k], out_a.at[k])
         core_a.append(go(out_a.at[k], in_a.at[k], partner))
+    mate.wait_recv()
+    theirs = st_c[...]
+    pair = merge([tall, theirs])
+    stat[1] = pair
+    to_x = [go(stat.at[1], st_x.at[i], x_peer(d)) for i, d in enumerate(XORDER)]
+    to_y = [go(stat.at[1], st_m.at[i], y_peer(d)) for i, d in enumerate(ORDER)]
+    to_z = [go(stat.at[1], st_n.at[i], z_peer(d)) for i, d in enumerate(ORDER)]
     for j in range(YL):
         split(others, wt_b[j], keep_b.at[j], out_b.at[j])
         core_b.append(go(out_b.at[j], in_b.at[j], partner))
     for j in range(NZ):
         split(others, wt_c[j], keep_c.at[j], out_c.at[j])
         core_c.append(go(out_c.at[j], in_c.at[j], partner))
+    both = columns_of([jnp.exp(p[0:1, :] - pair[0:1, :]) for p in (tall, theirs)])
+    both = both[0:HALF].reshape(YH, NX, PAD, 128)
+    f_own, f_in = both[..., 0:1], both[..., 1:2]
 
     def add_core(copy, keep, into, send):
         copy.wait_recv()
-        both = keep[...] + into[...].astype(F32)
-        keep[...] = both
-        send[...] = both.astype(BF16)
+        terms = keep[...] * f_own + into[...].astype(F32) * f_in
+        keep[...] = terms
+        send[...] = terms.astype(BF16)
 
     a_x = []
     for k in range(YL):
         add_core(core_a[k], keep_a.at[k], in_a.at[k], s1_a.at[k])
         a_x.append(wide_a(s1_a, r1_a, k))
-    for copy in to_y:
-        copy.wait_recv()
-    near = [st_y[i] for i in range(len(ORDER))]
-    plane = merge([group] + near)
-    stat[2] = plane
-    last = [go(stat.at[2], st_z.at[i], z_peer(d)) for i, d in enumerate(ORDER)]
+    for copy in to_x:
+        copy.wait_recv()
+    near_x = [st_x[i] for i in range(len(XORDER))]
+    line = merge([pair] + near_x)
+    stat[2] = line
+    along_y = [go(stat.at[2], st_y.at[i], y_peer(d)) for i, d in enumerate(ORDER)]
     for j in range(YL):
         add_core(core_b[j], keep_b.at[j], in_b.at[j], s1_b.at[j])
     b_y = wide_b(s1_b, r1_b)
@@ -292,7 +301,12 @@
         add_core(core_c[j], keep_c.at[j], in_c.at[j], s1_c.at[j])
     c_z = wide_c(s1_c, r1_c)
 
-    for copy in to_z + last:
+    for copy in along_y:
+        copy.wait_recv()
+    plane = merge([line] + [st_y[i] for i in range(len(ORDER))])
+    stat[4] = plane
+    along_z = [go(stat.at[4], st_z.at[i], z_peer(d)) for i, d in enumerate(ORDER)]
+    for copy in to_y + to_z + along_z:
         copy.wait_recv()
     whole = merge([plane] + [st_z[i] for i in range(len(ORDER))])
     highest, total = whole[0:1, :], whole[1:2, :] + whole[3:4, :]
@@ -304,19 +318,20 @@
         return jnp.exp(p[0:1, :] - highest) / total
 
     miss = (whole[1:2, :] / total).astype(BF16).astype(F32)
-    factors = columns_of([factor(group)] + [factor(p) for p in near]
-                         + [factor(st_m[i]) for i in range(len(ORDER))] + [miss])
+    near = near_x + [st_m[i] for i in range(len(ORDER))] + [st_n[i] for i in range(len(ORDER))]
+    factors = columns_of([factor(p) for p in [pair] + near] + [miss, factor(tall)])
     coef[...] = factors[0:HALF].reshape(YH, NX, PAD, 128)
-    probs = (shifted * factors[:, 0:1]).astype(BF16)
+    probs = (shifted * factors[:, MISS + 1:MISS + 2]).astype(BF16)
 
     a_y = []
     f_x = coef[:, x]
     for k in range(YL):
         for copy in a_x[k] + ta_x[k]:
             copy.wait_recv()
-        chunk = keep_a[k, :, x] + sum(r1_a[d, k].astype(F32) for d in XORDER)
+        chunk = keep_a[k, :, x] * f_x[..., 0:1]
+        chunk = chunk + sum(r1_a[d, k].astype(F32) * f_x[..., FROM_X + i:FROM_X + i + 1] for i, d in enumerate(XORDER))
         column = tk_a[k, :, x] + sum(tr_a[d, k] for d in XORDER)
-        chunk = chunk * f_x[..., 0:1] - column.astype(F32) * f_x[..., MISS:MISS + 1]
+        chunk = chunk - column.astype(F32) * f_x[..., MISS:MISS + 1]
         s2_a[k] = chunk.astype(BF16)
         if k == 0:
             keep_a[0, :, 0] = chunk
@@ -329,7 +344,7 @@
     f_y = coef[yh]
     column = tk_b[yl, yh] + sum(tr_b[d] for d in ORDER)
     sum_b = keep_b[yl, yh] * f_y[..., 0:1] - column.astype(F32) * f_y[..., MISS:MISS + 1]
-    sum_b = sum_b + sum(r1_b[d].astype(F32) * f_y[..., 1 + i:2 + i] for i, d in enumerate(ORDER))
+    sum_b = sum_b + sum(r1_b[d].astype(F32) * f_y[..., FROM_Y + i:FROM_Y + i + 1] for i, d in enumerate(ORDER))
     s2_b[...] = sum_b.astype(BF16)
     keep_b[0, 0] = sum_b
     b_x = [go(s2_b.at[(x + d) % NX], r2_b.at[d], x_peer(d)) for d in XORDER]
@@ -338,7 +353,7 @@
     f_z = coef[...]
     column = tk_c[z] + sum(tr_c[d] for d in ORDER)
     sum_c = keep_c[z] * f_z[..., 0:1] - column.astype(F32) * f_z[..., MISS:MISS + 1]
-    sum_c = sum_c + sum(r1_c[d].astype(F32) * f_z[..., 8 + i:9 + i] for i, d in enumerate(ORDER))
+    sum_c = sum_c + sum(r1_c[d].astype(F32) * f_z[..., FROM_Z + i:FROM_Z + i + 1] for i, d in enumerate(ORDER))
     s2_c[...] = sum_c.astype(BF16)
     keep_c[0] = sum_c
     c_x = [go(s2_c.at[:, (x + d) % NX], r2_c.at[d], x_peer(d)) for d in XORDER]
@@ -411,7 +426,8 @@
             v((2, PAD, 128), F32), v((PAD, 128), BF16), v((PAD, 128), BF16),
             v((NZ, PAD, 128), BF16), v((NY, PAD, 128), BF16),
             v((PAD, WA), F32), v((PAD, WB), F32), v((YH, PAD, WC), F32),
-            v((4, 8, TALL), F32), v((7, 8, TALL), F32), v((7, 8, TALL), F32), v((7, 8, TALL), F32), v((7, 8, TALL), F32),
+            v((5, 8, TALL), F32), v((8, TALL), F32), v((3, 8, TALL), F32),
+            v((7, 8, TALL), F32), v((7, 8, TALL), F32), v((7, 8, TALL), F32), v((7, 8, TALL), F32),
             v(halves + (128,), F32),
             v((YL,) + halves + (WA,), F32), v((YL,) + halves + (WB,), F32), v((NZ,) + halves + (WC,), F32),
             v((YL,) + halves + (WA,), BF16), v((YL,) + halves + (WB,), BF16), v((NZ,) + halves + (WC,), BF16),
@@ -426,7 +442,7 @@
             v((NY, PAD, WA), BF16), v((NX, PAD, WB), BF16), v((NX, YH, PAD, WC), BF16),
             v((NZ, PAD, 128), F32), v((NY, PAD, 128), F32), v((NZ, PAD, 128), F32), v((NY, PAD, 128), F32),
             v((YL, NZ, FA, VOCAB_DEV), BF16), v((YL, NZ, FB, VOCAB_DEV), BF16), v((NZ, YL, FC, VOCAB_DEV), BF16),
-            dma((12,)), dma((10,)), dma((256,)), dma((256,)),
+            dma((12,)), dma((10,)), dma((260,)), dma((260,)),
         ],
         compiler_params=pltpu.CompilerParams(
             collective_id=0, has_side_effects=True, vmem_limit_bytes=44 * 2**20),

time: 75.1 us -> 72.2 us (0.961)
  the two profiles are of different devices: /device:TPU:8 before, /device:TPU:6 now
where the time goes in v4:
time: 72.2 us; the launch traced here: 71.1 us
  Pallas kernels  66.8 us (93%)
  between operations  2.33 us (3%)
  local copies, waits for them, and re-layouts  2.01 us (3%)
    pallas_call x1, Pallas kernels, per_device(): pl.pallas_call(kernel, out_shape=(jax.ShapeDtypeStruct((1, 1), F32), jax....  66.8 us
    unnamed x2, local copies, waits for them, and re-layouts  2.01 us

profile of v4, /device:TPU:6, one launch (start us, length us, event | category | flops | bytes accessed | tf_op | source)
XLA Modules:
  0.0 71.1 jit_solution(15747727656269126544)
XLA Ops:
  0.6 66.8 %output_layer.1 = (f32[1,1]{1,0:T(1,128)}, bf16[4,8,144,256]{3,2,1,0:T(8,128)(2,1)S(1)}, bf16[13,144]{1,0:T(8,128)(2,1)S(1)}) custom-call(bf16[13,144]{1,0:T(8,128)(2,1)} %shard_hbm.1, bf16[4,8,144,256]{3,2,1,0:T(8,128)(2,1)} %bitcast.5, s32[1,208]{1,0:T(1,128)} %bitcast.6), custom_call_target="tpu_custom_call" | custom-call | tf_op jit(solution)/shard_map/output_layer/pallas_call | solution.py:412
  68.0 1.4 %copy.10 = bf16[4608,256]{1,0:T(8,128)(2,1)} copy(bf16[4608,256]{1,0:T(8,128)(2,1)S(1)} %bitcast.4) | data formatting | bytes 4718592
  69.4 0.6 copy.11

commit v5 on v4

v5 whole, which is shorter than its diff:
```python
import functools

import jax
import jax.numpy as jnp
from jax import lax
from jax.experimental import pallas as pl
from jax.experimental.pallas import tpu as pltpu
from jax.sharding import PartitionSpec as P

MESH = pl.DeviceIdType.MESH
F32 = jnp.float32
BF16 = jnp.bfloat16
NX, NY, NZ, NC = 4, 8, 8, 2
YH, YL = 2, 4
ROWS = 13
PAD = 16
FEATS = 144
FA, FB, FC = 80, 32, 32
WA, WB, WC = NZ * FA, NZ * FB, YL * FC
HALF = YH * NX * PAD
TALL = NC * HALF
D = YL * NZ * FEATS
VOCAB_DEV = 256
VOCAB_CHIP = NC * VOCAB_DEV
TOKENS = 208
ORDER = (1, 7, 2, 6, 3, 5, 4)
XORDER = (1, 3, 2)
FROM_X, FROM_Y, FROM_Z = 1, 4, 11
MISS = 18


def kernel(shard_hbm, weight_hbm, targets_hbm, loss, head_grad, hidden_grad,
           shard, targets, w_a, w_b, w_c, p_a, p_b, p_c, wt_a, wt_b, wt_c, hid_a, hid_b, hid_c, pad32,
           own_ab, own_c, z_rec, y_rec, line_a, line_b, line_c, stat, st_x, st_m, st_n, st_y, st_z, coef,
           keep_a, keep_b, keep_c, s1_a, s1_b, s1_c, r1_a, r1_b, r1_c, tk_a, tk_b, tk_c, tr_a, tr_b, tr_c,
           s2_a, s2_b, s2_c, r2_a, r2_b, r2_c, s3_ab, s3_c, r3_ab, r3_c, g_a, g_b, g_c, p_out, p_in, l_out,
           l_in, local, gsem, ssem, rsem):
    s = lax.axis_index("section")
    t = lax.axis_index("tp")
    x, yh, c = s // 4, (s // 2) % 2, s % 2
    yl, z = t // NZ, t % NZ
    y = yh * YL + yl

    def at(x_, y_, z_, c_):
        return {"section": x_ * 4 + (y_ // YL) * 2 + c_, "tp": (y_ % YL) * NZ + z_}

    def z_peer(d):
        return at(x, y, (z + d) % NZ, c)

    def y_peer(d):
        return at(x, (y + d) % NY, z, c)

    def x_peer(d):
        return at((x + d) % NX, y, z, c)

    sent = []

    def go(src, dst, peer):
        n = len(sent)
        copy = pltpu.make_async_remote_copy(
            src_ref=src, dst_ref=dst, send_sem=ssem.at[n], recv_sem=rsem.at[n], device_id=peer, device_id_type=MESH)
        copy.start()
        sent.append(copy)
        return copy

    peers = [z_peer(d) for d in ORDER] + [y_peer(d) for d in ORDER] + [x_peer(d) for d in XORDER]
    partner = at(x, y, z, 1 - c)
    peers.append(partner)
    barrier = pltpu.get_barrier_semaphore()
    for peer in peers:
        pl.semaphore_signal(barrier, inc=1, device_id=peer, device_id_type=MESH)

    fetch_small = [
        pltpu.make_async_copy(shard_hbm, shard, local.at[0]),
        pltpu.make_async_copy(targets_hbm, targets, local.at[1]),
    ]
    fetch = [
        pltpu.make_async_copy(weight_hbm.at[:, :, 0:FA], w_a, local.at[2]),
        pltpu.make_async_copy(weight_hbm.at[:, :, FA:FA + FB], w_b, local.at[3]),
    ] + [
        pltpu.make_async_copy(weight_hbm.at[:, i, FA + FB:FEATS], w_c.at[i], local.at[4 + i]) for i in range(NZ)
    ]
    for copy in fetch_small + fetch:
        copy.start()

    for copy in fetch_small:
        copy.wait()
    pad32[...] = jnp.zeros_like(pad32)
    pad32[0, 0:ROWS, 0:FA + FB] = shard[:, 0:FA + FB].astype(F32)
    pad32[1, 0:ROWS, 0:FC] = shard[:, FA + FB:FEATS].astype(F32)
    mine_ab, mine_c = pad32[0].astype(BF16), pad32[1].astype(BF16)
    own_ab[...] = mine_ab
    own_c[...] = mine_c

    row = lax.broadcasted_iota(jnp.int32, (HALF, TOKENS), 0)
    section = (row // PAD) % NX * 4 + row // (PAD * NX) * 2 + c
    match = (section * ROWS + row % PAD == lax.broadcasted_iota(jnp.int32, (HALF, TOKENS), 1)) & (row % PAD < ROWS)
    goal = jnp.sum(jnp.where(match, targets[...].astype(F32), 0.0), axis=1, keepdims=True).astype(jnp.int32)
    entry = lax.broadcasted_iota(jnp.int32, (HALF, VOCAB_CHIP), 1)
    mine = (s * (YL * NZ) + t) * VOCAB_DEV
    mate = ((s + 1 - 2 * c) * (YL * NZ) + t) * VOCAB_DEV
    hit = jnp.where(entry < VOCAB_DEV, entry + mine, entry + (mate - VOCAB_DEV)) == goal

    def dot(a, b, dims):
        return lax.dot_general(a, b, (dims, ((), ())), preferred_element_type=F32)

    nn, tn = ((1,), (0,)), ((0,), (0,))
    halves = (YH, NX, PAD)
    turn = [(yl + k) % YL for k in range(YL)]

    pl.semaphore_wait(barrier, len(peers))

    z_copies = [go(own_ab, z_rec.at[z], z_peer(d)) for d in ORDER]
    y_copies = [go(own_c, y_rec.at[y], y_peer(d)) for d in ORDER]
    z_rec[z] = mine_ab
    y_rec[y] = mine_c

    for copy in fetch:
        copy.wait()
    w_core = [go(src, dst, partner) for src, dst in ((w_a, p_a), (w_b, p_b), (w_c, p_c))]

    def transpose(parts, at_row):
        rows = pl.ds(at_row, VOCAB_DEV)
        for part, into in zip(parts, (wt_a, wt_b, wt_c)):
            for j in range(into.shape[0]):
                into[j, rows] = part[j].reshape(into.shape[2], VOCAB_DEV).T

    transpose((w_a, w_b, w_c), 0)
    for copy in z_copies:
        copy.wait_recv()
    for i in range(NZ):
        part = z_rec[i].astype(F32)
        line_a[:, FA * i:FA * (i + 1)] = part[:, 0:FA]
        line_b[:, FB * i:FB * (i + 1)] = part[:, FA:FA + FB]
    hid_a[yl, 0, yh, x] = line_a[...].astype(BF16)
    hid_b[yl, 0, yh, x] = line_b[...].astype(BF16)

    block = hid_a.at[yl, 0, yh, x]
    a_y = {d: go(block, block, y_peer(d)) for d in ORDER}
    block = hid_b.at[yl, 0, yh, x]
    b_x = [go(block, block, x_peer(d)) for d in XORDER]
    for copy in y_copies:
        copy.wait_recv()
    for i in range(NY):
        line_c[i // YL, :, FC * (i % YL):FC * (i % YL + 1)] = y_rec[i].astype(F32)[:, 0:FC]
    hid_c[z, 0, :, x] = line_c[...].astype(BF16)
    block = hid_c.at[z, 0, :, x]
    c_x = [go(block, block, x_peer(d)) for d in XORDER]

    a_x = []

    def pass_a(d):
        from_y = (y + NY - d) % NY
        block = hid_a.at[from_y % YL, 0, from_y // YL, x]
        a_x.extend([go(block, block, x_peer(dx)) for dx in XORDER])

    pass_a(0)
    for copy in b_x:
        copy.wait_recv()
    block = hid_b.at[yl, 0, yh]
    b_y = [go(block, block, y_peer(d)) for d in ORDER]
    for copy in c_x:
        copy.wait_recv()
    block = hid_c.at[z, 0]
    c_z = [go(block, block, z_peer(d)) for d in ORDER]
    for d in ORDER:
        a_y[d].wait_recv()
        pass_a(d)

    def wide_a(src, dst, k):
        return [go(src.at[k, :, (x + d) % NX], dst.at[d, k], x_peer(d)) for d in XORDER]

    def wide_b(src, dst):
        return [go(src.at[(y + d) % NY % YL, (y + d) % NY // YL], dst.at[d], y_peer(d)) for d in ORDER]

    def wide_c(src, dst):
        return [go(src.at[(z + d) % NZ], dst.at[d], z_peer(d)) for d in ORDER]

    for copy in w_core:
        copy.wait_recv()
    transpose((p_a, p_b, p_c), VOCAB_DEV)
    hot = hit.astype(F32).astype(BF16)
    for k in range(YL):
        tk_a[k] = dot(hot, wt_a[turn[k]], nn).astype(BF16).reshape(halves + (WA,))
    ta_x = [wide_a(tk_a, tr_a, k) for k in range(YL)]
    for j in range(YL):
        tk_b[j] = dot(hot, wt_b[j], nn).astype(BF16).reshape(halves + (WB,))
    for j in range(NZ):
        tk_c[j] = dot(hot, wt_c[j], nn).astype(BF16).reshape(halves + (WC,))

    def add_logits(sums, hid, parts):
        for j in range(hid.shape[0]):
            left = hid[j, 0].reshape(HALF, hid.shape[-1])
            sums = [so + dot(left, part[j].reshape(hid.shape[-1], VOCAB_DEV), nn) for so, part in zip(sums, parts)]
        return sums

    for copy in a_x:
        copy.wait_recv()
    sums = add_logits([jnp.zeros((HALF, VOCAB_DEV), F32)] * NC, hid_a, (w_a, p_a))
    for copy in b_y:
        copy.wait_recv()
    sums = add_logits(sums, hid_b, (w_b, p_b))
    for copy in c_z:
        copy.wait_recv()
    tb_y = wide_b(tk_b, tr_b)
    tc_z = wide_c(tk_c, tr_c)
    sums = add_logits(sums, hid_c, (w_c, p_c))
    logits = jnp.concatenate(sums, axis=1)

    top = jnp.max(logits, axis=1, keepdims=True)
    shifted = jnp.exp(logits - top)
    rest = jnp.sum(jnp.where(hit, 0.0, shifted), axis=1, keepdims=True)
    aim = jnp.sum(jnp.where(hit, shifted, 0.0), axis=1, keepdims=True)
    picked = jnp.sum(jnp.where(hit, logits, 0.0), axis=1, keepdims=True)
    others = jnp.where(hit, 0.0, shifted).astype(BF16)

    lane = lax.broadcasted_iota(jnp.int32, (HALF, 128), 1)
    columns = jnp.where(lane == 0, top, jnp.where(lane == 1, rest, jnp.where(lane == 2, picked, jnp.where(
        lane == 3, aim, 0.0))))
    tall = columns.T[0:8, :]
    stat[0] = tall

    def merge(parts):
        best = functools.reduce(jnp.maximum, [p[0:1, :] for p in parts])
        scale = [jnp.exp(p[0:1, :] - best) for p in parts]
        rest_ = sum(p[1:2, :] * f for p, f in zip(parts, scale))
        pick_ = sum(p[2:3, :] for p in parts)
        aim_ = sum(p[3:4, :] * f for p, f in zip(parts, scale))
        return jnp.concatenate([best, rest_, pick_, aim_, jnp.zeros((4, HALF), F32)], axis=0)

    def columns_of(rows):
        full = jnp.concatenate(rows + [jnp.zeros((128 - len(rows), HALF), F32)], axis=0)
        return full.T

    to_x = [go(stat.at[0], st_x.at[i], x_peer(d)) for i, d in enumerate(XORDER)]
    to_y = [go(stat.at[0], st_m.at[i], y_peer(d)) for i, d in enumerate(ORDER)]
    to_z = [go(stat.at[0], st_n.at[i], z_peer(d)) for i, d in enumerate(ORDER)]

    def term(weight, keep, send):
        terms = dot(others, weight, nn).reshape(keep.shape)
        keep[...] = terms
        send[...] = terms.astype(BF16)

    a_x = []
    for k in range(YL):
        term(wt_a[turn[k]], keep_a.at[k], s1_a.at[k])
        a_x.append(wide_a(s1_a, r1_a, k))
    for j in range(YL):
        term(wt_b[j], keep_b.at[j], s1_b.at[j])
    b_y = wide_b(s1_b, r1_b)
    for j in range(NZ):
        term(wt_c[j], keep_c.at[j], s1_c.at[j])
    c_z = wide_c(s1_c, r1_c)
    for copy in to_x:
        copy.wait_recv()
    near_x = [st_x[i] for i in range(len(XORDER))]
    line = merge([tall] + near_x)
    stat[1] = line
    along_y = [go(stat.at[1], st_y.at[i], y_peer(d)) for i, d in enumerate(ORDER)]
    h_core = [go(hid.at[:, 0], hid.at[:, 1], partner) for hid in (hid_a, hid_b, hid_c)]

    for copy in along_y:
        copy.wait_recv()
    plane = merge([line] + [st_y[i] for i in range(len(ORDER))])
    stat[2] = plane
    along_z = [go(stat.at[2], st_z.at[i], z_peer(d)) for i, d in enumerate(ORDER)]
    for copy in to_y + to_z + along_z:
        copy.wait_recv()
    whole = merge([plane] + [st_z[i] for i in range(len(ORDER))])
    highest, total = whole[0:1, :], whole[1:2, :] + whole[3:4, :]
    slot = lax.broadcasted_iota(jnp.int32, (1, HALF), 1)
    each = jnp.where(slot % PAD < ROWS, highest + jnp.log(total) - whole[2:3, :], 0.0)

    def factor(p):
        return jnp.exp(p[0:1, :] - highest) / total

    miss = (whole[1:2, :] / total).astype(BF16).astype(F32)
    near = near_x + [st_m[i] for i in range(len(ORDER))] + [st_n[i] for i in range(len(ORDER))]
    factors = columns_of([factor(p) for p in [tall] + near] + [miss])
    coef[...] = factors.reshape(halves + (128,))

    a_y = []
    f_x = coef[:, x]
    for k in range(YL):
        for copy in a_x[k] + ta_x[k]:
            copy.wait_recv()
        chunk = keep_a[k, :, x] * f_x[..., 0:1]
        chunk = chunk + sum(r1_a[d, k].astype(F32) * f_x[..., FROM_X + i:FROM_X + i + 1] for i, d in enumerate(XORDER))
        column = tk_a[k, :, x] + sum(tr_a[d, k] for d in XORDER)
        chunk = chunk - column.astype(F32) * f_x[..., MISS:MISS + 1]
        s2_a[k] = chunk.astype(BF16)
        if k == 0:
            keep_a[0, :, 0] = chunk
        for e in range(YH):
            if k or e:
                to = (yh + e) % YH
                a_y.append(go(s2_a.at[k, to], r2_a.at[e * YL + k], at(x, to * YL + turn[k], z, c)))
    for copy in b_y + tb_y:
        copy.wait_recv()
    f_y = coef[yh]
    column = tk_b[yl, yh] + sum(tr_b[d] for d in ORDER)
    sum_b = keep_b[yl, yh] * f_y[..., 0:1] - column.astype(F32) * f_y[..., MISS:MISS + 1]
    sum_b = sum_b + sum(r1_b[d].astype(F32) * f_y[..., FROM_Y + i:FROM_Y + i + 1] for i, d in enumerate(ORDER))
    s2_b[...] = sum_b.astype(BF16)
    keep_b[0, 0] = sum_b
    b_x = [go(s2_b.at[(x + d) % NX], r2_b.at[d], x_peer(d)) for d in XORDER]
    for copy in c_z + tc_z:
        copy.wait_recv()
    f_z = coef[...]
    column = tk_c[z] + sum(tr_c[d] for d in ORDER)
    sum_c = keep_c[z] * f_z[..., 0:1] - column.astype(F32) * f_z[..., MISS:MISS + 1]
    sum_c = sum_c + sum(r1_c[d].astype(F32) * f_z[..., FROM_Z + i:FROM_Z + i + 1] for i, d in enumerate(ORDER))
    s2_c[...] = sum_c.astype(BF16)
    keep_c[0] = sum_c
    c_x = [go(s2_c.at[:, (x + d) % NX], r2_c.at[d], x_peer(d)) for d in XORDER]

    probs = (shifted * factors[:, 0:1]).astype(BF16)
    p_out[...] = probs[:, VOCAB_DEV:VOCAB_CHIP]
    l_out[...] = jnp.concatenate([each, jnp.zeros((7, HALF), F32)], axis=0)
    swap = h_core + [go(p_out, p_in, partner), go(l_out, l_in, partner)]
    for copy in swap:
        copy.wait_recv()
    loss[0, 0] = (jnp.sum(each) + jnp.sum(l_in[0:1, :])) / TOKENS
    probs = jnp.concatenate([probs[:, 0:VOCAB_DEV], p_in[...]], axis=0)
    for hid, grad in ((hid_a, g_a), (hid_b, g_b), (hid_c, g_c)):
        for j in range(hid.shape[0]):
            left = hid[j].reshape(TALL, hid.shape[-1])
            grad[j] = dot(left, probs, tn).astype(BF16).reshape(grad.shape[1:])
    writes = [
        pltpu.make_async_copy(g_a, head_grad.at[:, :, 0:FA], gsem.at[0]),
        pltpu.make_async_copy(g_b, head_grad.at[:, :, FA:FA + FB], gsem.at[1]),
    ] + [
        pltpu.make_async_copy(g_c.at[i], head_grad.at[:, i, FA + FB:FEATS], gsem.at[2 + i]) for i in range(NZ)
    ]
    for write in writes:
        write.start()

    for copy in c_x:
        copy.wait_recv()
    part_c = keep_c[0, :, x] + sum(r2_c[d].astype(F32) for d in XORDER)
    for i in range(NY):
        s3_c[i, :, 0:FC] = part_c[i // YL, :, FC * (i % YL):FC * (i % YL + 1)]
    c_y = [go(s3_c.at[(y + d) % NY], r3_c.at[d], y_peer(d)) for d in ORDER]
    for copy in b_x:
        copy.wait_recv()
    part_b = keep_b[0, 0, x] + sum(r2_b[d].astype(F32) for d in XORDER)
    for copy in a_y:
        copy.wait_recv()
    part_a = keep_a[0, yh, 0] + sum(r2_a[n].astype(F32) for n in range(1, NY))
    for i in range(NZ):
        s3_ab[i, :, 0:FA] = part_a[:, FA * i:FA * (i + 1)]
        s3_ab[i, :, FA:FA + FB] = part_b[:, FB * i:FB * (i + 1)]
    ab_z = [go(s3_ab.at[(z + d) % NZ], r3_ab.at[d], z_peer(d)) for d in ORDER]
    for copy in c_y:
        copy.wait_recv()
    done_c = s3_c[y][:, 0:FC] + sum(r3_c[d][:, 0:FC] for d in ORDER)
    hidden_grad[:, FA + FB:FEATS] = done_c[0:ROWS].astype(BF16)
    for copy in ab_z:
        copy.wait_recv()
    done_ab = s3_ab[z][:, 0:FA + FB] + sum(r3_ab[d][:, 0:FA + FB] for d in ORDER)
    hidden_grad[:, 0:FA + FB] = done_ab[0:ROWS].astype(BF16)

    for copy in sent:
        copy.wait_send()
    for write in writes:
        write.wait()


def per_device(hidden, head_weight, targets):
    vmem = pl.BlockSpec(memory_space=pltpu.VMEM)
    hbm = pl.BlockSpec(memory_space=pltpu.HBM)
    v = pltpu.VMEM
    dma = pltpu.SemaphoreType.DMA
    halves = (YH, NX, PAD)
    loss, head_grad, hidden_grad = pl.pallas_call(
        kernel,
        out_shape=(
            jax.ShapeDtypeStruct((1, 1), F32),
            jax.ShapeDtypeStruct((YL, NZ, FEATS, VOCAB_DEV), BF16),
            jax.ShapeDtypeStruct((ROWS, FEATS), BF16),
        ),
        in_specs=[hbm, hbm, hbm],
        out_specs=(pl.BlockSpec(memory_space=pltpu.SMEM), pl.BlockSpec(memory_space=pl.ANY), vmem),
        scratch_shapes=[
            v((ROWS, FEATS), BF16), v((1, TOKENS), jnp.int32),
            v((YL, NZ, FA, VOCAB_DEV), BF16), v((YL, NZ, FB, VOCAB_DEV), BF16), v((NZ, YL, FC, VOCAB_DEV), BF16),
            v((YL, NZ, FA, VOCAB_DEV), BF16), v((YL, NZ, FB, VOCAB_DEV), BF16), v((NZ, YL, FC, VOCAB_DEV), BF16),
            v((YL, VOCAB_CHIP, WA), BF16), v((YL, VOCAB_CHIP, WB), BF16), v((NZ, VOCAB_CHIP, WC), BF16),
            v((YL, NC) + halves + (WA,), BF16), v((YL, NC) + halves + (WB,), BF16), v((NZ, NC) + halves + (WC,), BF16),
            v((2, PAD, 128), F32), v((PAD, 128), BF16), v((PAD, 128), BF16),
            v((NZ, PAD, 128), BF16), v((NY, PAD, 128), BF16),
            v((PAD, WA), F32), v((PAD, WB), F32), v((YH, PAD, WC), F32),
            v((3, 8, HALF), F32), v((3, 8, HALF), F32), v((7, 8, HALF), F32), v((7, 8, HALF), F32),
            v((7, 8, HALF), F32), v((7, 8, HALF), F32),
            v(halves + (128,), F32),
            v((YL,) + halves + (WA,), F32), v((YL,) + halves + (WB,), F32), v((NZ,) + halves + (WC,), F32),
            v((YL,) + halves + (WA,), BF16), v((YL,) + halves + (WB,), BF16), v((NZ,) + halves + (WC,), BF16),
            v((NX, YL, YH, PAD, WA), BF16), v((NY, NX, PAD, WB), BF16), v((NZ,) + halves + (WC,), BF16),
            v((YL,) + halves + (WA,), BF16), v((YL,) + halves + (WB,), BF16), v((NZ,) + halves + (WC,), BF16),
            v((NX, YL, YH, PAD, WA), BF16), v((NY, NX, PAD, WB), BF16), v((NZ,) + halves + (WC,), BF16),
            v((YL, YH, PAD, WA), BF16), v((NX, PAD, WB), BF16), v(halves + (WC,), BF16),
            v((NY, PAD, WA), BF16), v((NX, PAD, WB), BF16), v((NX, YH, PAD, WC), BF16),
            v((NZ, PAD, 128), F32), v((NY, PAD, 128), F32), v((NZ, PAD, 128), F32), v((NY, PAD, 128), F32),
            v((YL, NZ, FA, VOCAB_DEV), BF16), v((YL, NZ, FB, VOCAB_DEV), BF16), v((NZ, YL, FC, VOCAB_DEV), BF16),
            v((HALF, VOCAB_DEV), BF16), v((HALF, VOCAB_DEV), BF16), v((8, HALF), F32), v((8, HALF), F32),
            dma((12,)), dma((10,)), dma((192,)), dma((192,)),
        ],
        compiler_params=pltpu.CompilerParams(
            collective_id=0, has_side_effects=True, vmem_limit_bytes=44 * 2**20),
        name="output_layer",
    )(*[pltpu.with_memory_space_constraint(operand, pltpu.HBM) for operand in (
        hidden, head_weight.reshape(YL, NZ, FEATS, VOCAB_DEV), targets.reshape(1, TOKENS))])
    return loss.reshape(()), head_grad.reshape(D, VOCAB_DEV), hidden_grad


def solution(mesh):
    placed = (P("section", "tp"), P(None, ("section", "tp")), P())
    return jax.shard_map(
        per_device,
        mesh=mesh,
        in_specs=placed,
        out_specs=(P(), P(None, ("section", "tp")), P("section", "tp")),
        check_vma=False,
    )
```

time: 72.2 us -> 68.7 us (0.952)
  Pallas kernels: 66.8 us -> 63.9 us
    pallas_call x1, Pallas kernels: 66.8 us -> 63.9 us  [per_device(): pl.pallas_call(kernel, out_shape=(jax.ShapeDtypeStruct((1, 1), F32), jax....]
where the time goes in v5:
time: 68.7 us; the launch traced here: 68.2 us
  Pallas kernels  63.9 us (93%)
  between operations  2.33 us (3%)
  local copies, waits for them, and re-layouts  2.01 us (3%)
    pallas_call x1, Pallas kernels, per_device(): pl.pallas_call(kernel, out_shape=(jax.ShapeDtypeStruct((1, 1), F32), jax....  63.9 us
    unnamed x2, local copies, waits for them, and re-layouts  2.01 us

profile of v5, /device:TPU:6, one launch (start us, length us, event | category | flops | bytes accessed | tf_op | source)
XLA Modules:
  0.0 68.2 jit_solution(17052056455994343860)
XLA Ops:
  0.6 63.9 %output_layer.1 = (f32[1,1]{1,0:T(1,128)}, bf16[4,8,144,256]{3,2,1,0:T(8,128)(2,1)S(1)}, bf16[13,144]{1,0:T(8,128)(2,1)S(1)}) custom-call(bf16[13,144]{1,0:T(8,128)(2,1)} %shard_hbm.1, bf16[4,8,144,256]{3,2,1,0:T(8,128)(2,1)} %bitcast.5, s32[1,208]{1,0:T(1,128)} %bitcast.6), custom_call_target="tpu_custom_call" | custom-call | tf_op jit(solution)/shard_map/output_layer/pallas_call | solution.py:375
  65.0 1.4 %copy.10 = bf16[4608,256]{1,0:T(8,128)(2,1)} copy(bf16[4608,256]{1,0:T(8,128)(2,1)S(1)} %bitcast.4) | data formatting | bytes 4718592
  66.5 0.6 copy.11

commit v6 on v5

--- a/solution.py
+++ b/solution.py
@@ -25,15 +25,15 @@
 TOKENS = 208
 ORDER = (1, 7, 2, 6, 3, 5, 4)
 XORDER = (1, 3, 2)
-FROM_X, FROM_Y, FROM_Z = 1, 4, 11
-MISS = 18
+OWN = NY + NX + NX
+MISS = OWN + 1
 
 
 def kernel(shard_hbm, weight_hbm, targets_hbm, loss, head_grad, hidden_grad,
            shard, targets, w_a, w_b, w_c, p_a, p_b, p_c, wt_a, wt_b, wt_c, hid_a, hid_b, hid_c, pad32,
-           own_ab, own_c, z_rec, y_rec, line_a, line_b, line_c, stat, st_x, st_m, st_n, st_y, st_z, coef,
+           own_ab, own_c, z_rec, y_rec, line_a, line_b, line_c, stat, st_x, st_m, st_n, st_b, st_c, st_y, st_z, coef,
            keep_a, keep_b, keep_c, s1_a, s1_b, s1_c, r1_a, r1_b, r1_c, tk_a, tk_b, tk_c, tr_a, tr_b, tr_c,
-           s2_a, s2_b, s2_c, r2_a, r2_b, r2_c, s3_ab, s3_c, r3_ab, r3_c, g_a, g_b, g_c, p_out, p_in, l_out,
+           t2_a, t2_b, t2_c, t3_a, t3_b, t3_c, s2_a, s2_b, s2_c, r2_a, r2_b, r2_c, s3_ab, s3_c, r3_ab, r3_c, g_a, g_b, g_c, p_out, p_in, l_out,
            l_in, local, gsem, ssem, rsem):
     s = lax.axis_index("section")
     t = lax.axis_index("tp")
@@ -126,6 +126,18 @@
                 into[j, rows] = part[j].reshape(into.shape[2], VOCAB_DEV).T
 
     transpose((w_a, w_b, w_c), 0)
+
+    hot = hit.astype(F32).astype(BF16)
+
+    def columns_at(first):
+        rows = pl.ds(first, VOCAB_DEV)
+        for into, weight in ((tk_a, wt_a), (tk_b, wt_b), (tk_c, wt_c)):
+            for j in range(into.shape[0]):
+                chunk = turn[j] if weight is wt_a else j
+                column = dot(hot[:, first:first + VOCAB_DEV], weight[chunk, rows], nn).astype(BF16).reshape(into.shape[1:])
+                into[j] = into[j] + column if first else column
+
+    columns_at(0)
     for copy in z_copies:
         copy.wait_recv()
     for i in range(NZ):
@@ -163,6 +175,10 @@
         copy.wait_recv()
     block = hid_c.at[z, 0]
     c_z = [go(block, block, z_peer(d)) for d in ORDER]
+    for copy in w_core:
+        copy.wait_recv()
+    transpose((p_a, p_b, p_c), VOCAB_DEV)
+    columns_at(VOCAB_DEV)
     for d in ORDER:
         a_y[d].wait_recv()
         pass_a(d)
@@ -176,17 +192,7 @@
     def wide_c(src, dst):
         return [go(src.at[(z + d) % NZ], dst.at[d], z_peer(d)) for d in ORDER]
 
-    for copy in w_core:
-        copy.wait_recv()
-    transpose((p_a, p_b, p_c), VOCAB_DEV)
-    hot = hit.astype(F32).astype(BF16)
-    for k in range(YL):
-        tk_a[k] = dot(hot, wt_a[turn[k]], nn).astype(BF16).reshape(halves + (WA,))
     ta_x = [wide_a(tk_a, tr_a, k) for k in range(YL)]
-    for j in range(YL):
-        tk_b[j] = dot(hot, wt_b[j], nn).astype(BF16).reshape(halves + (WB,))
-    for j in range(NZ):
-        tk_c[j] = dot(hot, wt_c[j], nn).astype(BF16).reshape(halves + (WC,))
 
     def add_logits(sums, hid, parts):
         for j in range(hid.shape[0]):
@@ -253,71 +259,125 @@
     c_z = wide_c(s1_c, r1_c)
     for copy in to_x:
         copy.wait_recv()
-    near_x = [st_x[i] for i in range(len(XORDER))]
-    line = merge([tall] + near_x)
+    line = merge([tall] + [st_x[i] for i in range(len(XORDER))])
     stat[1] = line
-    along_y = [go(stat.at[1], st_y.at[i], y_peer(d)) for i, d in enumerate(ORDER)]
+    y_turn = [(e, k, at(x, (yh + e) % YH * YL + turn[k], z, c)) for e in range(YH) for k in range(YL) if e or k]
+    along_y = [go(stat.at[1], st_y.at[e * YL + k], peer) for e, k, peer in y_turn]
     h_core = [go(hid.at[:, 0], hid.at[:, 1], partner) for hid in (hid_a, hid_b, hid_c)]
 
+    def second_a(src, dst, k):
+        return [go(src.at[k, (yh + e) % YH], dst.at[e * YL + k], peer) for e, k_, peer in y_turn if k_ == k]
+
+    def second_b(src, dst):
+        return [go(src.at[(x + d) % NX], dst.at[d], x_peer(d)) for d in XORDER]
+
+    def second_c(src, dst):
+        return [go(src.at[:, (x + d) % NX], dst.at[d], x_peer(d)) for d in XORDER]
+
+    ta_y = []
+    for k in range(YL):
+        for copy in ta_x[k]:
+            copy.wait_recv()
+        t2_a[k] = tk_a[k, :, x] + sum(tr_a[d, k] for d in XORDER)
+        ta_y += second_a(t2_a, t3_a, k)
+    for copy in tb_y:
+        copy.wait_recv()
+    t2_b[...] = tk_b[yl, yh] + sum(tr_b[d] for d in ORDER)
+    tb_x = second_b(t2_b, t3_b)
+    for copy in tc_z:
+        copy.wait_recv()
+    t2_c[...] = tk_c[z] + sum(tr_c[d] for d in ORDER)
+    tc_x = second_c(t2_c, t3_c)
+
+    for copy in to_y + to_z:
+        copy.wait_recv()
+    near_y, near_z = ([tall] + [st[i] for i in range(len(ORDER))] for st in (st_m, st_n))
+    line_y, line_z = merge(near_y), merge(near_z)
+    stat[2] = line_y
+    stat[3] = line_z
+    tiles_x = [go(stat.at[2], st_b.at[i], x_peer(d)) for i, d in enumerate(XORDER)]
+    tiles_x += [go(stat.at[3], st_c.at[i], x_peer(d)) for i, d in enumerate(XORDER)]
+
+    def ratios(parts, best):
+        return [jnp.exp(p[0:1, :] - best[0:1, :]) for p in parts]
+
+    near_x = [tall] + [st_x[i] for i in range(len(XORDER))]
+    scales = ratios(near_x, line) + ratios(near_y, line_y) + ratios(near_z, line_z)
+    coef[...] = columns_of(scales).reshape(halves + (128,))
+
+    def scaled(own, others_, f, first):
+        parts = [own] + [other.astype(F32) for other in others_]
+        return sum(p * f[..., first + i:first + i + 1] for i, p in enumerate(parts))
+
+    a_y = []
+    f_x = coef[:, x]
+    for k in range(YL):
+        for copy in a_x[k]:
+            copy.wait_recv()
+        chunk = scaled(keep_a[k, :, x], [r1_a[d, k] for d in XORDER], f_x, 0)
+        s2_a[k] = chunk.astype(BF16)
+        if k == 0:
+            keep_a[0, :, 0] = chunk
+        a_y += second_a(s2_a, r2_a, k)
     for copy in along_y:
         copy.wait_recv()
-    plane = merge([line] + [st_y[i] for i in range(len(ORDER))])
-    stat[2] = plane
-    along_z = [go(stat.at[2], st_z.at[i], z_peer(d)) for i, d in enumerate(ORDER)]
-    for copy in to_y + to_z + along_z:
+    lines = [line] + [st_y[n] for n in range(1, NY)]
+    plane = merge(lines)
+    stat[4] = plane
+    along_z = [go(stat.at[4], st_z.at[i], z_peer(d)) for i, d in enumerate(ORDER)]
+    for copy in b_y:
+        copy.wait_recv()
+    sum_b = scaled(keep_b[yl, yh], [r1_b[d] for d in ORDER], coef[yh], NX)
+    s2_b[...] = sum_b.astype(BF16)
+    keep_b[0, 0] = sum_b
+    b_x = second_b(s2_b, r2_b)
+    for copy in c_z:
+        copy.wait_recv()
+    sum_c = scaled(keep_c[z], [r1_c[d] for d in ORDER], coef[...], NX + NY)
+    s2_c[...] = sum_c.astype(BF16)
+    keep_c[0] = sum_c
+    c_x = second_c(s2_c, r2_c)
+
+    for copy in tiles_x + along_z:
         copy.wait_recv()
     whole = merge([plane] + [st_z[i] for i in range(len(ORDER))])
     highest, total = whole[0:1, :], whole[1:2, :] + whole[3:4, :]
     slot = lax.broadcasted_iota(jnp.int32, (1, HALF), 1)
     each = jnp.where(slot % PAD < ROWS, highest + jnp.log(total) - whole[2:3, :], 0.0)
-
-    def factor(p):
-        return jnp.exp(p[0:1, :] - highest) / total
-
     miss = (whole[1:2, :] / total).astype(BF16).astype(F32)
-    near = near_x + [st_m[i] for i in range(len(ORDER))] + [st_n[i] for i in range(len(ORDER))]
-    factors = columns_of([factor(p) for p in [tall] + near] + [miss])
+    lines_y = [line_y] + [st_b[i] for i in range(len(XORDER))]
+    lines_z = [line_z] + [st_c[i] for i in range(len(XORDER))]
+    factors = columns_of([f / total for f in ratios(lines + lines_y + lines_z + [tall], whole)] + [miss])
     coef[...] = factors.reshape(halves + (128,))
-
-    a_y = []
-    f_x = coef[:, x]
-    for k in range(YL):
-        for copy in a_x[k] + ta_x[k]:
-            copy.wait_recv()
-        chunk = keep_a[k, :, x] * f_x[..., 0:1]
-        chunk = chunk + sum(r1_a[d, k].astype(F32) * f_x[..., FROM_X + i:FROM_X + i + 1] for i, d in enumerate(XORDER))
-        column = tk_a[k, :, x] + sum(tr_a[d, k] for d in XORDER)
-        chunk = chunk - column.astype(F32) * f_x[..., MISS:MISS + 1]
-        s2_a[k] = chunk.astype(BF16)
-        if k == 0:
-            keep_a[0, :, 0] = chunk
-        for e in range(YH):
-            if k or e:
-                to = (yh + e) % YH
-                a_y.append(go(s2_a.at[k, to], r2_a.at[e * YL + k], at(x, to * YL + turn[k], z, c)))
-    for copy in b_y + tb_y:
-        copy.wait_recv()
-    f_y = coef[yh]
-    column = tk_b[yl, yh] + sum(tr_b[d] for d in ORDER)
-    sum_b = keep_b[yl, yh] * f_y[..., 0:1] - column.astype(F32) * f_y[..., MISS:MISS + 1]
-    sum_b = sum_b + sum(r1_b[d].astype(F32) * f_y[..., FROM_Y + i:FROM_Y + i + 1] for i, d in enumerate(ORDER))
-    s2_b[...] = sum_b.astype(BF16)
-    keep_b[0, 0] = sum_b
-    b_x = [go(s2_b.at[(x + d) % NX], r2_b.at[d], x_peer(d)) for d in XORDER]
-    for copy in c_z + tc_z:
-        copy.wait_recv()
-    f_z = coef[...]
-    column = tk_c[z] + sum(tr_c[d] for d in ORDER)
-    sum_c = keep_c[z] * f_z[..., 0:1] - column.astype(F32) * f_z[..., MISS:MISS + 1]
-    sum_c = sum_c + sum(r1_c[d].astype(F32) * f_z[..., FROM_Z + i:FROM_Z + i + 1] for i, d in enumerate(ORDER))
-    s2_c[...] = sum_c.astype(BF16)
-    keep_c[0] = sum_c
-    c_x = [go(s2_c.at[:, (x + d) % NX], r2_c.at[d], x_peer(d)) for d in XORDER]
-
-    probs = (shifted * factors[:, 0:1]).astype(BF16)
+    probs = (shifted * factors[:, OWN:OWN + 1]).astype(BF16)
     p_out[...] = probs[:, VOCAB_DEV:VOCAB_CHIP]
     l_out[...] = jnp.concatenate([each, jnp.zeros((7, HALF), F32)], axis=0)
     swap = h_core + [go(p_out, p_in, partner), go(l_out, l_in, partner)]
+
+    for copy in c_x + tc_x:
+        copy.wait_recv()
+    f_c, f_ab = coef[:, x], coef[yh, x]
+    part_c = scaled(keep_c[0, :, x], [r2_c[d] for d in XORDER], f_c, NY + NX)
+    column = t2_c[:, x] + sum(t3_c[d] for d in XORDER)
+    part_c = part_c - column.astype(F32) * f_c[..., MISS:MISS + 1]
+    for i in range(NY):
+        s3_c[i, :, 0:FC] = part_c[i // YL, :, FC * (i % YL):FC * (i % YL + 1)]
+    c_y = [go(s3_c.at[(y + d) % NY], r3_c.at[d], y_peer(d)) for d in ORDER]
+    for copy in b_x + tb_x:
+        copy.wait_recv()
+    part_b = scaled(keep_b[0, 0, x], [r2_b[d] for d in XORDER], f_ab, NY)
+    column = t2_b[x] + sum(t3_b[d] for d in XORDER)
+    part_b = part_b - column.astype(F32) * f_ab[..., MISS:MISS + 1]
+    for copy in a_y + ta_y:
+        copy.wait_recv()
+    part_a = scaled(keep_a[0, yh, 0], [r2_a[n] for n in range(1, NY)], f_ab, 0)
+    column = t2_a[0, yh] + sum(t3_a[n] for n in range(1, NY))
+    part_a = part_a - column.astype(F32) * f_ab[..., MISS:MISS + 1]
+    for i in range(NZ):
+        s3_ab[i, :, 0:FA] = part_a[:, FA * i:FA * (i + 1)]
+        s3_ab[i, :, FA:FA + FB] = part_b[:, FB * i:FB * (i + 1)]
+    ab_z = [go(s3_ab.at[(z + d) % NZ], r3_ab.at[d], z_peer(d)) for d in ORDER]
+
     for copy in swap:
         copy.wait_recv()
     loss[0, 0] = (jnp.sum(each) + jnp.sum(l_in[0:1, :])) / TOKENS
@@ -335,22 +395,6 @@
     for write in writes:
         write.start()
 
-    for copy in c_x:
-        copy.wait_recv()
-    part_c = keep_c[0, :, x] + sum(r2_c[d].astype(F32) for d in XORDER)
-    for i in range(NY):
-        s3_c[i, :, 0:FC] = part_c[i // YL, :, FC * (i % YL):FC * (i % YL + 1)]
-    c_y = [go(s3_c.at[(y + d) % NY], r3_c.at[d], y_peer(d)) for d in ORDER]
-    for copy in b_x:
-        copy.wait_recv()
-    part_b = keep_b[0, 0, x] + sum(r2_b[d].astype(F32) for d in XORDER)
-    for copy in a_y:
-        copy.wait_recv()
-    part_a = keep_a[0, yh, 0] + sum(r2_a[n].astype(F32) for n in range(1, NY))
-    for i in range(NZ):
-        s3_ab[i, :, 0:FA] = part_a[:, FA * i:FA * (i + 1)]
-        s3_ab[i, :, FA:FA + FB] = part_b[:, FB * i:FB * (i + 1)]
-    ab_z = [go(s3_ab.at[(z + d) % NZ], r3_ab.at[d], z_peer(d)) for d in ORDER]
     for copy in c_y:
         copy.wait_recv()
     done_c = s3_c[y][:, 0:FC] + sum(r3_c[d][:, 0:FC] for d in ORDER)
@@ -390,8 +434,8 @@
             v((2, PAD, 128), F32), v((PAD, 128), BF16), v((PAD, 128), BF16),
             v((NZ, PAD, 128), BF16), v((NY, PAD, 128), BF16),
             v((PAD, WA), F32), v((PAD, WB), F32), v((YH, PAD, WC), F32),
-            v((3, 8, HALF), F32), v((3, 8, HALF), F32), v((7, 8, HALF), F32), v((7, 8, HALF), F32),
-            v((7, 8, HALF), F32), v((7, 8, HALF), F32),
+            v((5, 8, HALF), F32), v((3, 8, HALF), F32), v((7, 8, HALF), F32), v((7, 8, HALF), F32),
+            v((3, 8, HALF), F32), v((3, 8, HALF), F32), v((NY, 8, HALF), F32), v((7, 8, HALF), F32),
             v(halves + (128,), F32),
             v((YL,) + halves + (WA,), F32), v((YL,) + halves + (WB,), F32), v((NZ,) + halves + (WC,), F32),
             v((YL,) + halves + (WA,), BF16), v((YL,) + halves + (WB,), BF16), v((NZ,) + halves + (WC,), BF16),
@@ -400,10 +444,12 @@
             v((NX, YL, YH, PAD, WA), BF16), v((NY, NX, PAD, WB), BF16), v((NZ,) + halves + (WC,), BF16),
             v((YL, YH, PAD, WA), BF16), v((NX, PAD, WB), BF16), v(halves + (WC,), BF16),
             v((NY, PAD, WA), BF16), v((NX, PAD, WB), BF16), v((NX, YH, PAD, WC), BF16),
+            v((YL, YH, PAD, WA), BF16), v((NX, PAD, WB), BF16), v(halves + (WC,), BF16),
+            v((NY, PAD, WA), BF16), v((NX, PAD, WB), BF16), v((NX, YH, PAD, WC), BF16),
             v((NZ, PAD, 128), F32), v((NY, PAD, 128), F32), v((NZ, PAD, 128), F32), v((NY, PAD, 128), F32),
             v((YL, NZ, FA, VOCAB_DEV), BF16), v((YL, NZ, FB, VOCAB_DEV), BF16), v((NZ, YL, FC, VOCAB_DEV), BF16),
             v((HALF, VOCAB_DEV), BF16), v((HALF, VOCAB_DEV), BF16), v((8, HALF), F32), v((8, HALF), F32),
-            dma((12,)), dma((10,)), dma((192,)), dma((192,)),
+            dma((12,)), dma((10,)), dma((208,)), dma((208,)),
         ],
         compiler_params=pltpu.CompilerParams(
             collective_id=0, has_side_effects=True, vmem_limit_bytes=44 * 2**20),

time: 68.7 us -> 69 us (level)
  no operation moved by 1% of the time
where the time goes in v6:
time: 69 us; the launch traced here: 68.8 us
  Pallas kernels  64.5 us (93%)
  between operations  2.33 us (3%)
  local copies, waits for them, and re-layouts  2.01 us (3%)
    pallas_call x1, Pallas kernels, per_device(): pl.pallas_call(kernel, out_shape=(jax.ShapeDtypeStruct((1, 1), F32), jax....  64.5 us
    unnamed x2, local copies, waits for them, and re-layouts  2.01 us

profile of v6, /device:TPU:6, one launch (start us, length us, event | category | flops | bytes accessed | tf_op | source)
XLA Modules:
  0.0 68.8 jit_solution(4381889349892839070)
XLA Ops:
  0.6 64.5 %output_layer.1 = (f32[1,1]{1,0:T(1,128)}, bf16[4,8,144,256]{3,2,1,0:T(8,128)(2,1)S(1)}, bf16[13,144]{1,0:T(8,128)(2,1)S(1)}) custom-call(bf16[13,144]{1,0:T(8,128)(2,1)} %shard_hbm.1, bf16[4,8,144,256]{3,2,1,0:T(8,128)(2,1)} %bitcast.5, s32[1,208]{1,0:T(1,128)} %bitcast.6), custom_call_target="tpu_custom_call" | custom-call | tf_op jit(solution)/shard_map/output_layer/pallas_call | solution.py:419
  65.7 1.4 %copy.10 = bf16[4608,256]{1,0:T(8,128)(2,1)} copy(bf16[4608,256]{1,0:T(8,128)(2,1)S(1)} %bitcast.4) | data formatting | bytes 4718592
  67.1 0.6 copy.11

commit v7 on v6

--- a/solution.py
+++ b/solution.py
@@ -31,10 +31,11 @@
 
 def kernel(shard_hbm, weight_hbm, targets_hbm, loss, head_grad, hidden_grad,
            shard, targets, w_a, w_b, w_c, p_a, p_b, p_c, wt_a, wt_b, wt_c, hid_a, hid_b, hid_c, pad32,
-           own_ab, own_c, z_rec, y_rec, line_a, line_b, line_c, stat, st_x, st_m, st_n, st_b, st_c, st_y, st_z, coef,
-           keep_a, keep_b, keep_c, s1_a, s1_b, s1_c, r1_a, r1_b, r1_c, tk_a, tk_b, tk_c, tr_a, tr_b, tr_c,
-           t2_a, t2_b, t2_c, t3_a, t3_b, t3_c, s2_a, s2_b, s2_c, r2_a, r2_b, r2_c, s3_ab, s3_c, r3_ab, r3_c, g_a, g_b, g_c, p_out, p_in, l_out,
-           l_in, local, gsem, ssem, rsem):
+           own_ab, own_c, z_rec, y_rec, line_a, line_b, line_c, stat, st_x, st_m, st_n, st_b, st_c, st_y,
+           st_z, coef, keep_a, keep_b, keep_c, s1_a, s1_b, s1_c, r1_a, r1_b, r1_c, tk_a, tk_b, tk_c, to_a,
+           to_b, to_c, ti_a, ti_b, ti_c, tr_a, tr_b, tr_c, t2_a, t2_b, t2_c, t3_a, t3_b, t3_c, s2_a, s2_b,
+           s2_c, r2_a, r2_b, r2_c, s3_ab, s3_c, r3_ab, r3_c, g_a, g_b, g_c, p_out, p_in, l_out, l_in, local,
+           gsem, ssem, rsem):
     s = lax.axis_index("section")
     t = lax.axis_index("tp")
     x, yh, c = s // 4, (s // 2) % 2, s % 2
@@ -92,14 +93,15 @@
     own_ab[...] = mine_ab
     own_c[...] = mine_c
 
-    row = lax.broadcasted_iota(jnp.int32, (HALF, TOKENS), 0)
-    section = (row // PAD) % NX * 4 + row // (PAD * NX) * 2 + c
-    match = (section * ROWS + row % PAD == lax.broadcasted_iota(jnp.int32, (HALF, TOKENS), 1)) & (row % PAD < ROWS)
+    row = lax.broadcasted_iota(jnp.int32, (TALL, TOKENS), 0)
+    section = (row // PAD) % NX * 4 + (row // (PAD * NX)) % YH * 2 + (row // HALF + c) % 2
+    match = (section * ROWS + row % PAD == lax.broadcasted_iota(jnp.int32, (TALL, TOKENS), 1)) & (row % PAD < ROWS)
     goal = jnp.sum(jnp.where(match, targets[...].astype(F32), 0.0), axis=1, keepdims=True).astype(jnp.int32)
-    entry = lax.broadcasted_iota(jnp.int32, (HALF, VOCAB_CHIP), 1)
     mine = (s * (YL * NZ) + t) * VOCAB_DEV
     mate = ((s + 1 - 2 * c) * (YL * NZ) + t) * VOCAB_DEV
-    hit = jnp.where(entry < VOCAB_DEV, entry + mine, entry + (mate - VOCAB_DEV)) == goal
+    hot = lax.broadcasted_iota(jnp.int32, (TALL, VOCAB_DEV), 1) + mine == goal
+    entry = lax.broadcasted_iota(jnp.int32, (HALF, VOCAB_CHIP), 1)
+    hit = jnp.where(entry < VOCAB_DEV, entry + mine, entry + (mate - VOCAB_DEV)) == goal[0:HALF]
 
     def dot(a, b, dims):
         return lax.dot_general(a, b, (dims, ((), ())), preferred_element_type=F32)
@@ -117,8 +119,6 @@
 
     for copy in fetch:
         copy.wait()
-    w_core = [go(src, dst, partner) for src, dst in ((w_a, p_a), (w_b, p_b), (w_c, p_c))]
-
     def transpose(parts, at_row):
         rows = pl.ds(at_row, VOCAB_DEV)
         for part, into in zip(parts, (wt_a, wt_b, wt_c)):
@@ -127,17 +127,22 @@
 
     transpose((w_a, w_b, w_c), 0)
 
-    hot = hit.astype(F32).astype(BF16)
-
-    def columns_at(first):
-        rows = pl.ds(first, VOCAB_DEV)
-        for into, weight in ((tk_a, wt_a), (tk_b, wt_b), (tk_c, wt_c)):
-            for j in range(into.shape[0]):
-                chunk = turn[j] if weight is wt_a else j
-                column = dot(hot[:, first:first + VOCAB_DEV], weight[chunk, rows], nn).astype(BF16).reshape(into.shape[1:])
-                into[j] = into[j] + column if first else column
-
-    columns_at(0)
+    hot = hot.astype(F32).astype(BF16)
+    t_core = []
+    for keep, out, into, weight in ((tk_c, to_c, ti_c, wt_c), (tk_a, to_a, ti_a, wt_a), (tk_b, to_b, ti_b, wt_b)):
+        for j in range(keep.shape[0]):
+            chunk = turn[j] if weight is wt_a else j
+            column = dot(hot, weight[chunk, 0:VOCAB_DEV], nn).astype(BF16)
+            keep[j] = column[0:HALF].reshape(keep.shape[1:])
+            out[j] = column[HALF:TALL].reshape(keep.shape[1:])
+        t_core.append(go(out, into, partner))
+    w_core = [go(src, dst, partner) for src, dst in ((w_a, p_a), (w_b, p_b), (w_c, p_c))]
+
+    def both_columns(copy, keep, into):
+        copy.wait_recv()
+        for j in range(keep.shape[0]):
+            keep[j] = keep[j] + into[j]
+
     for copy in z_copies:
         copy.wait_recv()
     for i in range(NZ):
@@ -167,6 +172,21 @@
         a_x.extend([go(block, block, x_peer(dx)) for dx in XORDER])
 
     pass_a(0)
+
+    def wide_a(src, dst, k):
+        return [go(src.at[k, :, (x + d) % NX], dst.at[d, k], x_peer(d)) for d in XORDER]
+
+    def wide_b(src, dst):
+        return [go(src.at[(y + d) % NY % YL, (y + d) % NY // YL], dst.at[d], y_peer(d)) for d in ORDER]
+
+    def wide_c(src, dst):
+        return [go(src.at[(z + d) % NZ], dst.at[d], z_peer(d)) for d in ORDER]
+
+    both_columns(t_core[0], tk_c, ti_c)
+    tc_z = wide_c(tk_c, tr_c)
+    both_columns(t_core[1], tk_a, ti_a)
+    ta_x = [wide_a(tk_a, tr_a, k) for k in range(YL)]
+
     for copy in b_x:
         copy.wait_recv()
     block = hid_b.at[yl, 0, yh]
@@ -175,24 +195,15 @@
         copy.wait_recv()
     block = hid_c.at[z, 0]
     c_z = [go(block, block, z_peer(d)) for d in ORDER]
-    for copy in w_core:
-        copy.wait_recv()
-    transpose((p_a, p_b, p_c), VOCAB_DEV)
-    columns_at(VOCAB_DEV)
+    both_columns(t_core[2], tk_b, ti_b)
+    tb_y = wide_b(tk_b, tr_b)
     for d in ORDER:
         a_y[d].wait_recv()
         pass_a(d)
 
-    def wide_a(src, dst, k):
-        return [go(src.at[k, :, (x + d) % NX], dst.at[d, k], x_peer(d)) for d in XORDER]
-
-    def wide_b(src, dst):
-        return [go(src.at[(y + d) % NY % YL, (y + d) % NY // YL], dst.at[d], y_peer(d)) for d in ORDER]
-
-    def wide_c(src, dst):
-        return [go(src.at[(z + d) % NZ], dst.at[d], z_peer(d)) for d in ORDER]
-
-    ta_x = [wide_a(tk_a, tr_a, k) for k in range(YL)]
+    for copy in w_core:
+        copy.wait_recv()
+    transpose((p_a, p_b, p_c), VOCAB_DEV)
 
     def add_logits(sums, hid, parts):
         for j in range(hid.shape[0]):
@@ -208,8 +219,6 @@
     sums = add_logits(sums, hid_b, (w_b, p_b))
     for copy in c_z:
         copy.wait_recv()
-    tb_y = wide_b(tk_b, tr_b)
-    tc_z = wide_c(tk_c, tr_c)
     sums = add_logits(sums, hid_c, (w_c, p_c))
     logits = jnp.concatenate(sums, axis=1)
 
@@ -441,6 +450,8 @@
             v((YL,) + halves + (WA,), BF16), v((YL,) + halves + (WB,), BF16), v((NZ,) + halves + (WC,), BF16),
             v((NX, YL, YH, PAD, WA), BF16), v((NY, NX, PAD, WB), BF16), v((NZ,) + halves + (WC,), BF16),
             v((YL,) + halves + (WA,), BF16), v((YL,) + halves + (WB,), BF16), v((NZ,) + halves + (WC,), BF16),
+            v((YL,) + halves + (WA,), BF16), v((YL,) + halves + (WB,), BF16), v((NZ,) + halves + (WC,), BF16),
+            v((YL,) + halves + (WA,), BF16), v((YL,) + halves + (WB,), BF16), v((NZ,) + halves + (WC,), BF16),
             v((NX, YL, YH, PAD, WA), BF16), v((NY, NX, PAD, WB), BF16), v((NZ,) + halves + (WC,), BF16),
             v((YL, YH, PAD, WA), BF16), v((NX, PAD, WB), BF16), v(halves + (WC,), BF16),
             v((NY, PAD, WA), BF16), v((NX, PAD, WB), BF16), v((NX, YH, PAD, WC), BF16),

time: 69 us -> 68.5 us (level); the launches traced: 68.8 us -> 67.3 us
  Pallas kernels: 64.5 us -> 63 us
    pallas_call x1, Pallas kernels: 64.5 us -> 63 us  [per_device(): pl.pallas_call(kernel, out_shape=(jax.ShapeDtypeStruct((1, 1), F32), jax....]
where the time goes in v7:
time: 68.5 us; the launch traced here: 67.3 us
  Pallas kernels  63 us (92%)
  between operations  2.33 us (3%)
  local copies, waits for them, and re-layouts  2.01 us (3%)
    pallas_call x1, Pallas kernels, per_device(): pl.pallas_call(kernel, out_shape=(jax.ShapeDtypeStruct((1, 1), F32), jax....  63 us
    unnamed x2, local copies, waits for them, and re-layouts  2.01 us

profile of v7, /device:TPU:6, one launch (start us, length us, event | category | flops | bytes accessed | tf_op | source)
XLA Modules:
  0.0 67.3 jit_solution(9590895798566509005)
XLA Ops:
  0.6 63.0 %output_layer.1 = (f32[1,1]{1,0:T(1,128)}, bf16[4,8,144,256]{3,2,1,0:T(8,128)(2,1)S(1)}, bf16[13,144]{1,0:T(8,128)(2,1)S(1)}) custom-call(bf16[13,144]{1,0:T(8,128)(2,1)} %shard_hbm.1, bf16[4,8,144,256]{3,2,1,0:T(8,128)(2,1)} %bitcast.5, s32[1,208]{1,0:T(1,128)} %bitcast.6), custom_call_target="tpu_custom_call" | custom-call | tf_op jit(solution)/shard_map/output_layer/pallas_call | solution.py:428
  64.2 1.4 %copy.10 = bf16[4608,256]{1,0:T(8,128)(2,1)} copy(bf16[4608,256]{1,0:T(8,128)(2,1)S(1)} %bitcast.4) | data formatting | bytes 4718592
  65.6 0.6 copy.11

commit v8 on v7

--- a/solution.py
+++ b/solution.py
@@ -182,25 +182,25 @@
     def wide_c(src, dst):
         return [go(src.at[(z + d) % NZ], dst.at[d], z_peer(d)) for d in ORDER]
 
+
+    for copy in b_x:
+        copy.wait_recv()
+    block = hid_b.at[yl, 0, yh]
+    b_y = [go(block, block, y_peer(d)) for d in ORDER]
+    for copy in c_x:
+        copy.wait_recv()
+    block = hid_c.at[z, 0]
+    c_z = [go(block, block, z_peer(d)) for d in ORDER]
+    for d in ORDER:
+        a_y[d].wait_recv()
+        pass_a(d)
+
     both_columns(t_core[0], tk_c, ti_c)
     tc_z = wide_c(tk_c, tr_c)
     both_columns(t_core[1], tk_a, ti_a)
     ta_x = [wide_a(tk_a, tr_a, k) for k in range(YL)]
-
-    for copy in b_x:
-        copy.wait_recv()
-    block = hid_b.at[yl, 0, yh]
-    b_y = [go(block, block, y_peer(d)) for d in ORDER]
-    for copy in c_x:
-        copy.wait_recv()
-    block = hid_c.at[z, 0]
-    c_z = [go(block, block, z_peer(d)) for d in ORDER]
     both_columns(t_core[2], tk_b, ti_b)
     tb_y = wide_b(tk_b, tr_b)
-    for d in ORDER:
-        a_y[d].wait_recv()
-        pass_a(d)
-
     for copy in w_core:
         copy.wait_recv()
     transpose((p_a, p_b, p_c), VOCAB_DEV)

time: 68.5 us -> 65.7 us (0.959)
  Pallas kernels: 63 us -> 60.7 us
    pallas_call x1, Pallas kernels: 63 us -> 60.7 us  [per_device(): pl.pallas_call(kernel, out_shape=(jax.ShapeDtypeStruct((1, 1), F32), jax....]
where the time goes in v8:
time: 65.7 us; the launch traced here: 65.1 us
  Pallas kernels  60.7 us (92%)
  between operations  2.33 us (4%)
  local copies, waits for them, and re-layouts  2.01 us (3%)
    pallas_call x1, Pallas kernels, per_device(): pl.pallas_call(kernel, out_shape=(jax.ShapeDtypeStruct((1, 1), F32), jax....  60.7 us
    unnamed x2, local copies, waits for them, and re-layouts  2.01 us

profile of v8, /device:TPU:6, one launch (start us, length us, event | category | flops | bytes accessed | tf_op | source)
XLA Modules:
  0.0 65.1 jit_solution(9665116589186363859)
XLA Ops:
  0.6 60.7 %output_layer.1 = (f32[1,1]{1,0:T(1,128)}, bf16[4,8,144,256]{3,2,1,0:T(8,128)(2,1)S(1)}, bf16[13,144]{1,0:T(8,128)(2,1)S(1)}) custom-call(bf16[13,144]{1,0:T(8,128)(2,1)} %shard_hbm.1, bf16[4,8,144,256]{3,2,1,0:T(8,128)(2,1)} %bitcast.5, s32[1,208]{1,0:T(1,128)} %bitcast.6), custom_call_target="tpu_custom_call" | custom-call | tf_op jit(solution)/shard_map/output_layer/pallas_call | solution.py:428
  61.9 1.4 %copy.10 = bf16[4608,256]{1,0:T(8,128)(2,1)} copy(bf16[4608,256]{1,0:T(8,128)(2,1)S(1)} %bitcast.4) | data formatting | bytes 4718592
  63.3 0.6 copy.11

commit v9 on v8

--- a/solution.py
+++ b/solution.py
@@ -358,10 +358,6 @@
     lines_z = [line_z] + [st_c[i] for i in range(len(XORDER))]
     factors = columns_of([f / total for f in ratios(lines + lines_y + lines_z + [tall], whole)] + [miss])
     coef[...] = factors.reshape(halves + (128,))
-    probs = (shifted * factors[:, OWN:OWN + 1]).astype(BF16)
-    p_out[...] = probs[:, VOCAB_DEV:VOCAB_CHIP]
-    l_out[...] = jnp.concatenate([each, jnp.zeros((7, HALF), F32)], axis=0)
-    swap = h_core + [go(p_out, p_in, partner), go(l_out, l_in, partner)]
 
     for copy in c_x + tc_x:
         copy.wait_recv()
@@ -387,6 +383,10 @@
         s3_ab[i, :, FA:FA + FB] = part_b[:, FB * i:FB * (i + 1)]
     ab_z = [go(s3_ab.at[(z + d) % NZ], r3_ab.at[d], z_peer(d)) for d in ORDER]
 
+    probs = (shifted * factors[:, OWN:OWN + 1]).astype(BF16)
+    p_out[...] = probs[:, VOCAB_DEV:VOCAB_CHIP]
+    l_out[...] = jnp.concatenate([each, jnp.zeros((7, HALF), F32)], axis=0)
+    swap = h_core + [go(p_out, p_in, partner), go(l_out, l_in, partner)]
     for copy in swap:
         copy.wait_recv()
     loss[0, 0] = (jnp.sum(each) + jnp.sum(l_in[0:1, :])) / TOKENS

time: 65.7 us -> 65.6 us (level)
  no operation moved by 1% of the time
where the time goes in v9:
time: 65.6 us; the launch traced here: 65 us
  Pallas kernels  60.7 us (93%)
  between operations  2.33 us (4%)
  local copies, waits for them, and re-layouts  2.01 us (3%)
    pallas_call x1, Pallas kernels, per_device(): pl.pallas_call(kernel, out_shape=(jax.ShapeDtypeStruct((1, 1), F32), jax....  60.7 us
    unnamed x2, local copies, waits for them, and re-layouts  2.01 us

profile of v9, /device:TPU:6, one launch (start us, length us, event | category | flops | bytes accessed | tf_op | source)
XLA Modules:
  0.0 65.0 jit_solution(3619836807176573882)
XLA Ops:
  0.6 60.7 %output_layer.1 = (f32[1,1]{1,0:T(1,128)}, bf16[4,8,144,256]{3,2,1,0:T(8,128)(2,1)S(1)}, bf16[13,144]{1,0:T(8,128)(2,1)S(1)}) custom-call(bf16[13,144]{1,0:T(8,128)(2,1)} %shard_hbm.1, bf16[4,8,144,256]{3,2,1,0:T(8,128)(2,1)} %bitcast.5, s32[1,208]{1,0:T(1,128)} %bitcast.6), custom_call_target="tpu_custom_call" | custom-call | tf_op jit(solution)/shard_map/output_layer/pallas_call | solution.py:428
  61.8 1.4 %copy.10 = bf16[4608,256]{1,0:T(8,128)(2,1)} copy(bf16[4608,256]{1,0:T(8,128)(2,1)S(1)} %bitcast.4) | data formatting | bytes 4718592
  63.3 0.6 copy.11
